TPU v7x, 256 devices: a whole 4x4x8 slice. The times are simulated.
256 devices in a mesh: section: 4 (over y), grp: 4 (over x), tp: 16 (over z, core).
Axes of the slice: x: 4, y: 4, z: 8, core: 2. Of those that a mesh axis runs over, the one named last changes fastest.
Arguments:
- ctx_latent: bfloat16 [48, 1024, 512], P(('section', 'grp'), 'tp'), may hold values from -4 to 4
- ctx_rope: bfloat16 [48, 512, 128], P(('section', 'grp'), 'tp'), may hold values from -4 to 4
- ctx_scale: bfloat16 [48, 1024, 4], P(('section', 'grp'), 'tp'), may hold values from 0.5 to 2
- dest: int32 [48], replicated, may hold values from 0 to 3, as said below
- ctx_len: int32 [48], P(('section', 'grp')), may hold values from 256 to 1024
- queries: bfloat16 [48, 32, 36864], P(('section', 'grp'), None, 'tp'), may hold values from -100 to 100
- reply_keys: bfloat16 [48, 8, 2304], P(('section', 'grp')), may hold values from -4 to 4
- reply_len: int32 [48, 8], P(('section', 'grp')), may hold values from 1 to 4
- targets: int32 [48, 32], P(('section', 'grp')), may hold values from 0 to 4095
- w_uv: bfloat16 [512, 8192], P(None, 'tp'), may hold values from -0.25 to 0.25
- w_out: bfloat16 [8192, 7168], P('tp'), may hold values from -0.0625 to 0.0625
- w_vocab: bfloat16 [7168, 4096], P(None, 'tp')
Outputs:
- scores: float32 [48, 8], P(('section', 'grp'))
Inputs may be any that keep to these rules, and one draw needn't show every extreme that they name: `dest`: within each row of section, every decode group receives exactly 3 requests; one prefill group sends at most 2 requests to one decode group, and some prefill group sends 2 to one decode group in every draw.
All inputs are finite; a program needn't handle non-finite values.
Results may differ from a plain program's by a relative error of at most 0.0037.
Values may be sent and summed in bfloat16 or wider, within the bound.
A program may use at most 128 MiB of HBM per device.

v0:
```python
import jax
import jax.numpy as jnp
from jax import lax
from jax.sharding import PartitionSpec as P

KVR = 512
ROPE = 64
BLK = 128
SLOTS = 2


softmax_scale = 192.0 ** (-0.5)
norm_epsilon = 1e-06


def from_behind(value, axis, steps):
    count = lax.axis_size(axis)
    pairs = [(source, (source + steps) % count) for source in range(count)]
    return lax.ppermute(value, axis, pairs)


def merged_2(value, axis, join):
    pieces = jax.tree.map(lambda part: lax.all_gather(part, axis), value)
    head = jax.tree.map(lambda part: part[0], pieces)
    tail = jax.tree.map(lambda part: part[1:], pieces)
    running, _ = lax.scan(lambda running, section: (join(running, section), None), head, tail)
    return running


def select_rows(arrays, row_index, is_valid):
    result = []
    for array in arrays:
        chosen = jnp.take(array, row_index, axis=0)
        shape_mask = is_valid.reshape((is_valid.shape[0],) + (1,) * (array.ndim - 1))
        result.append(jnp.where(shape_mask, chosen, jnp.zeros_like(chosen)))
    return tuple(result)


def first_valid(slot_flags, wanted):
    running = jnp.cumsum(slot_flags.astype(jnp.int32)) - 1
    choose = jnp.logical_and(
        slot_flags[None, :], running[None, :] == jnp.arange(wanted, dtype=jnp.int32)[:, None]
    )
    return jnp.sum(
        choose.astype(jnp.int32) * jnp.arange(slot_flags.shape[0], dtype=jnp.int32)[None, :], axis=1
    )


def normalize(hidden):
    return (
        hidden * lax.rsqrt(jnp.mean(hidden * hidden, axis=1, keepdims=True) + norm_epsilon)
    ).astype(jnp.bfloat16)


def combine_totals(earlier, later):
    joint_top = jnp.maximum(earlier[0], later[0])
    joint_total = earlier[1] * jnp.exp(earlier[0] - joint_top) + later[1] * jnp.exp(
        later[0] - joint_top
    )
    return (joint_top, joint_total, earlier[2] + later[2])


def per_device(
    ctx_latent,
    ctx_rope,
    ctx_scale,
    dest,
    ctx_len,
    queries,
    reply_keys,
    reply_len,
    targets,
    w_uv,
    w_out,
    w_vocab,
):
    section_count = lax.axis_size("section")
    group_count = lax.axis_size("grp")
    requests = ctx_latent.shape[0]
    moved = from_behind((ctx_latent, ctx_rope, ctx_scale), "section", 1)
    source_section = (lax.axis_index("section") + section_count - 1) % section_count
    own_group = lax.axis_index("grp")
    section_dest = lax.dynamic_slice_in_dim(
        dest, source_section * group_count * requests, group_count * requests
    )
    section_dest = section_dest.reshape(group_count, requests)
    local_dest = lax.dynamic_index_in_dim(section_dest, own_group, 0, keepdims=False)
    positions = jnp.arange(requests, dtype=jnp.int32)
    earlier = jnp.logical_and(
        local_dest[:, None] == local_dest[None, :], positions[:, None] > positions[None, :]
    )
    ranks = jnp.sum(earlier.astype(jnp.int32), axis=1)
    slot_ids = local_dest * SLOTS + ranks
    slot_range = jnp.arange(group_count * SLOTS, dtype=jnp.int32)
    matches = slot_ids[None, :] == slot_range[:, None]
    send_index = jnp.sum(matches.astype(jnp.int32) * positions[None, :], axis=1)
    send_valid = jnp.any(matches, axis=1)
    outgoing = select_rows(moved, send_index, send_valid)
    incoming = (
        lax.all_to_all(outgoing[0], "grp", split_axis=0, concat_axis=0, tiled=True),
        lax.all_to_all(outgoing[1], "grp", split_axis=0, concat_axis=0, tiled=True),
        lax.all_to_all(outgoing[2], "grp", split_axis=0, concat_axis=0, tiled=True),
    )
    arriving = jnp.sum((section_dest == own_group).astype(jnp.int32), axis=1)
    slot_flags = (jnp.arange(SLOTS, dtype=jnp.int32)[None, :] < arriving[:, None]).reshape(
        group_count * SLOTS
    )
    keep_index = first_valid(slot_flags, requests)
    spread = (
        lax.all_gather(incoming[0], "tp", axis=1, tiled=True),
        lax.all_gather(incoming[1], "tp", axis=1, tiled=True),
        lax.all_gather(incoming[2], "tp", axis=1, tiled=True),
    )
    latent = jnp.take(spread[0], keep_index, axis=0)
    rope_keys = jnp.take(spread[1], keep_index, axis=0)
    scales = jnp.take(spread[2], keep_index, axis=0)
    context = latent.shape[1]
    scaled = (
        latent.reshape(requests, context, KVR // BLK, BLK).astype(jnp.float32)
        * scales.astype(jnp.float32)[:, :, :, None]
    )
    dequant = scaled.reshape(requests, context, KVR).astype(jnp.bfloat16)
    rope_flat = rope_keys.reshape(requests, context, ROPE)
    heads_local = queries.shape[2] // (KVR + ROPE)
    cand = reply_len.shape[1]
    steps = targets.shape[1] // cand
    query = queries.reshape(requests, cand, steps, heads_local, KVR + ROPE)
    reply = reply_keys.reshape(requests, cand, steps, KVR + ROPE)
    context_scores = jnp.einsum(
        "rathk,rpk->rathp", query[..., :KVR], dequant, preferred_element_type=jnp.float32
    )
    context_scores = context_scores + jnp.einsum(
        "rathk,rpk->rathp", query[..., KVR:], rope_flat, preferred_element_type=jnp.float32
    )
    context_scores = context_scores * softmax_scale
    visible = jnp.arange(context, dtype=jnp.int32)[None, :] < ctx_len[:, None]
    context_scores = jnp.where(visible[:, None, None, None, :], context_scores, -jnp.inf)
    reply_scores = (
        jnp.einsum("rathk,rauk->rathu", query, reply, preferred_element_type=jnp.float32)
        * softmax_scale
    )
    causal = (
        jnp.arange(steps, dtype=jnp.int32)[None, :] <= jnp.arange(steps, dtype=jnp.int32)[:, None]
    )
    reply_scores = jnp.where(causal[None, None, :, None, :], reply_scores, -jnp.inf)
    row_top = jnp.maximum(jnp.max(context_scores, axis=4), jnp.max(reply_scores, axis=4))[..., None]
    context_exp = jnp.exp(context_scores - row_top)
    reply_exp = jnp.exp(reply_scores - row_top)
    row_total = jnp.sum(context_exp, axis=4, keepdims=True) + jnp.sum(
        reply_exp, axis=4, keepdims=True
    )
    context_weight = (context_exp / row_total).astype(jnp.bfloat16)
    reply_weight = (reply_exp / row_total).astype(jnp.bfloat16)
    attended = jnp.einsum(
        "rathp,rpk->rathk", context_weight, dequant, preferred_element_type=jnp.float32
    )
    attended = attended + jnp.einsum(
        "rathu,rauk->rathk", reply_weight, reply[..., :KVR], preferred_element_type=jnp.float32
    )
    attended = attended.astype(jnp.bfloat16)
    head_value = jnp.einsum(
        "rathk,khv->rathv",
        attended,
        w_uv.reshape(KVR, heads_local, -1),
        preferred_element_type=jnp.float32,
    )
    row_count = requests * cand * steps
    flat_values = head_value.astype(jnp.bfloat16).reshape(row_count, -1)
    hidden = lax.psum(jnp.dot(flat_values, w_out, preferred_element_type=jnp.float32), "tp")
    normed = normalize(hidden)
    logits = jnp.dot(normed, w_vocab, preferred_element_type=jnp.float32)
    vocab_local = w_vocab.shape[1]
    vocab_offset = lax.axis_index("tp") * vocab_local
    flat_targets = targets.reshape(row_count)
    local_top = jnp.max(logits, axis=1)
    local_total = jnp.sum(jnp.exp(logits - local_top[:, None]), axis=1)
    target_hit = (
        jnp.arange(vocab_local, dtype=jnp.int32)[None, :] + vocab_offset == flat_targets[:, None]
    )
    target_logit = jnp.sum(jnp.where(target_hit, logits, 0.0), axis=1)
    merged = merged_2((local_top, local_total, target_logit), "tp", combine_totals)
    log_prob = (merged[2] - (merged[0] + jnp.log(merged[1]))).reshape(requests, cand, steps)
    inside = jnp.arange(steps, dtype=jnp.int32)[None, None, :] < reply_len[:, :, None]
    return jnp.sum(jnp.where(inside, log_prob, 0.0), axis=2) / reply_len.astype(jnp.float32)


def solution(mesh):
    placed = (
        P(("section", "grp"), "tp", None),
        P(("section", "grp"), "tp", None),
        P(("section", "grp"), "tp", None),
        P(),
        P(("section", "grp")),
        P(("section", "grp"), None, "tp"),
        P(("section", "grp"), None, None),
        P(("section", "grp"), None),
        P(("section", "grp"), None),
        P(None, "tp"),
        P("tp", None),
        P(None, "tp"),
    )
    return jax.shard_map(
        per_device,
        mesh=mesh,
        in_specs=placed,
        out_specs=P(("section", "grp"), None),
        check_vma=False,
    )
```

profile of v0, /device:TPU:1, one launch (start us, length us, event | category | flops | bytes accessed | tf_op | source)
XLA Modules:
  0.0 321.4 jit_solution(17530254530395183435)
XLA Ops:
  6.6 2.2 collective-permute-start.2
  8.8 0.7 dynamic_slice.17
  10.0 1.6 collective-permute-done.2
  12.3 8.4 %all_to_all.15 = bf16[8,32,128]{2,1,0:T(8,128)(2,1)} all-to-all(bf16[8,32,128]{2,1,0:T(8,128)(2,1)S(1)} %select_select_fusion.1), channel_id=1, replica_groups=mesh['section'=4,'grp'=4,'tp'=16] {'grp'}, dimensions={0} | all-to-all | bytes 131072 | tf_op jit(solution)/shard_map/all_to_all | solution.py:101
  20.9 5.9 %collective-permute-done = bf16[3,64,512]{2,1,0:T(8,128)(2,1)S(1)} collective-permute-done((bf16[3,64,512]{2,1,0:T(8,128)(2,1)}, bf16[3,64,512]{2,1,0:T(8,128)(2,1)S(1)}, u32[]{:S(2)}, u32[]{:S(2)}) %collective-permute-start) | collective-permute-done | bytes 196640 | tf_op jit(solution)/shard_map/ppermute | solution.py:19
  27.5 10.0 %all_to_all.16 = bf16[8,64,512]{2,1,0:T(8,128)(2,1)} all-to-all(bf16[8,64,512]{2,1,0:T(8,128)(2,1)S(1)} %select_select_fusion), channel_id=1, replica_groups=mesh['section'=4,'grp'=4,'tp'=16] {'grp'}, dimensions={0} | all-to-all | bytes 1048576 | tf_op jit(solution)/shard_map/all_to_all | solution.py:100
  39.2 2.7 fusion.62
  42.7 0.7 reshape.281
  43.3 3.2 all-to-all-start.1
  46.6 0.8 reshape.195
  47.6 0.9 reshape.196
  48.5 2.1 all-to-all-done.1
  50.8 31.9 %all_gather.28 = bf16[8,1024,4]{0,2,1:T(4,128)(2,1)S(1)} all-gather(bf16[8,64,4]{0,2,1:T(4,128)(2,1)S(1)} %copy.66), channel_id=1, replica_groups=mesh['section'=4,'grp'=4,'tp'=16] {'tp'}, dimensions={1}, use_global_device_ids=true | all-gather | bytes 69632 | tf_op jit(solution)/shard_map/all_gather | solution.py:112
  82.7 0.6 copy.67
  84.5 5.5 %mul.74 = f32[3,1024,4,128]{3,2,1,0:T(4,128)} broadcast(f32[3,1024,4]{2,1,0:T(8,128)S(1)} %copy.68), dimensions={0,1,2} | broadcast | bytes 6340608 | tf_op jit(solution)/shard_map/mul | solution.py:119
  90.0 7.9 %mul.75 = f32[3,1024,512]{2,1,0:T(8,128)} reshape(f32[3,1024,4,128]{3,2,1,0:T(4,128)} %mul.74) | data formatting | bytes 12582912 | tf_op jit(solution)/shard_map/mul | solution.py:119
  97.9 1.9 gather_fusion.5
  100.2 1.6 fusion.33
  101.8 17.5 %all-gather.6.cloned.1.call-done = bf16[8,1024,512]{2,1,0:T(8,128)(2,1)} async-done(((bf16[8,64,512]{2,1,0:T(8,128)(2,1)}), bf16[8,1024,512]{2,1,0:T(8,128)(2,1)}) %all-gather.6.cloned.1.call-update) | async-done | bytes 8388624 | tf_op jit(solution)/shard_map/all_gather | solution.py:110
  119.4 5.9 %gather_fusion.1 = bf16[3,1024,512]{2,1,0:T(8,128)(2,1)} fusion(bf16[8,1024,512]{2,1,0:T(8,128)(2,1)} %all-gather.6.cloned.1.call-done, s32[1024]{0:T(1024)S(1)} %pad_clamp_fusion), kind=kCustom, calls=%fused_computation.1 | custom fusion | bytes 6291468 | tf_op jit(solution)/shard_map/jit(_take)/gather | solution.py:114
  125.2 5.0 %multiply_convert_fusion = bf16[3,1024,512]{2,1,0:T(8,128)(2,1)S(1)} fusion(f32[3,1024,512]{2,1,0:T(8,128)} %mul.75, bf16[3,1024,512]{2,1,0:T(8,128)(2,1)} %gather_fusion.1, pred[3]{0:T(512)(128)(4,1)S(1)} %compare_and_fusion.1), kind=kLoop, calls=%fused_computation.16 | loop fusion | flops 6291456 | bytes 12582915 | tf_op jit(solution)/shard_map/convert_element_type | solution.py:122
  130.2 2.3 bitcast_reduce_fusion
  133.1 1.8 fusion.14
  135.0 2.2 fusion.45
  137.2 3.0 fusion.30
  140.3 5.9 %fusion.46 = f32[96,7168]{1,0:T(8,128)} fusion(bf16[512,7168]{1,0:T(8,128)(2,1)} %param.24, bf16[12,8,4,128]{3,2,1,0:T(4,128)(2,1)S(1)} %bitcast.102), kind=kOutput, calls=%fused_computation.53 | convolution fusion | flops 704643072 | bytes 10190848 | tf_op jit(solution)/shard_map/dot_general | solution.py:169
  146.3 0.6 copy-done.7
  148.1 112.5 %all-reduce.6.cloned.1.call-done = f32[96,7168]{1,0:T(8,128)} async-done(((f32[96,7168]{1,0:T(8,128)}), f32[96,7168]{1,0:T(8,128)}) %all-reduce.6.cloned.1.call-update) | async-done | bytes 2752528 | tf_op jit(solution)/shard_map/psum | solution.py:169
  260.7 2.2 multiply_reduce_fusion
  263.3 2.9 fusion.63
  267.2 45.7 %all-reduce.3 = (f32[1536]{0:T(1024)S(1)}, f32[1536]{0:T(1024)S(1)}, f32[1536]{0:T(1024)S(1)}) all-reduce(f32[1536]{0:T(1024)S(1)} %dynamic-update-slice, f32[1536]{0:T(1024)S(1)} %dynamic-update-slice.1, f32[1536]{0:T(1024)S(1)} %dynamic-update-slice.2), channel_id=2, replica_groups=mesh['section'=4,'grp'=4,'tp'=16] {'tp'}, use_global_device_ids=true, to_apply=%add | all-reduce | flops 4608 | bytes 36864
  313.4 0.7 while.14
  (117 shorter events, 10.8 us)
Async XLA Ops:
  6.5 31.1 %copy-start.9 = (bf16[3,64,4]{1,2,0:T(4,128)(2,1)S(1)}, bf16[3,64,4]{1,2,0:T(4,128)(2,1)}, u32[]{:S(2)}) copy-start(bf16[3,64,4]{1,2,0:T(4,128)(2,1)} %param.16) | copy-start | bytes 4612
  6.5 31.7 %copy-start.4 = (bf16[3,32,2304]{2,1,0:T(8,128)(2,1)S(1)}, bf16[3,32,2304]{2,1,0:T(8,128)(2,1)}, u32[]{:S(2)}) copy-start(bf16[3,32,2304]{2,1,0:T(8,128)(2,1)} %param.19) | copy-start | bytes 1327108
  6.5 32.3 %copy-start.5 = (bf16[3,8,2304]{2,1,0:T(8,128)(2,1)S(1)}, bf16[3,8,2304]{2,1,0:T(8,128)(2,1)}, u32[]{:S(2)}) copy-start(bf16[3,8,2304]{2,1,0:T(8,128)(2,1)} %param.20) | copy-start | bytes 331780
  6.5 32.6 %copy-start.8 = (s32[3]{0:T(128)S(1)}, s32[3]{0:T(128)}, u32[]{:S(2)}) copy-start(s32[3]{0:T(128)} %param.18) | copy-start | bytes 40
  6.5 91.4 %all-gather.8.cloned.1.call-start = ((), (), s32[]{:S(2)}) async-start(), calls=%async_computation.4 | async-start | bytes 1114112 | tf_op jit(solution)/shard_map/all_gather | solution.py:111
  6.6 5.1 %collective-permute-start.2 = (bf16[3,32,128]{2,1,0:T(8,128)(2,1)}, bf16[3,32,128]{2,1,0:T(8,128)(2,1)S(1)}, u32[]{:S(2)}, u32[]{:S(2)}) collective-permute-start(bf16[3,32,128]{2,1,0:T(8,128)(2,1)} %param.15), channel_id=1, source_target_pairs={{0,64},{64,128},{128,192},{192,0},{1,65},{65,129},{129,193},{193,1... | collective-permute-start | bytes 73736 | tf_op jit(solution)/shard_map/ppermute | solution.py:19
  20.7 98.6 %all-gather.6.cloned.1.call-start = ((), (), s32[]{:S(2)}) async-start(), calls=%async_computation.3 | async-start | bytes 8912896 | tf_op jit(solution)/shard_map/all_gather | solution.py:110
  20.8 6.0 %collective-permute-start = (bf16[3,64,512]{2,1,0:T(8,128)(2,1)}, bf16[3,64,512]{2,1,0:T(8,128)(2,1)S(1)}, u32[]{:S(2)}, u32[]{:S(2)}) collective-permute-start(bf16[3,64,512]{2,1,0:T(8,128)(2,1)} %param.14), channel_id=1, source_target_pairs={{0,64},{64,128},{128,192},{192,0},{1,65},{65,129},{129,193},{193,1... | collective-permute-start | bytes 589832 | tf_op jit(solution)/shard_map/ppermute | solution.py:19
  37.6 10.0 %copy-start.3 = (bf16[512,512]{1,0:T(8,128)(2,1)S(1)}, bf16[512,512]{1,0:T(8,128)(2,1)}, u32[]{:S(2)}) copy-start(bf16[512,512]{1,0:T(8,128)(2,1)} %param.23) | copy-start | bytes 1572868
  37.6 4.4 %collective-permute-start.1 = (bf16[3,64,4]{1,2,0:T(4,128)(2,1)S(1)}, bf16[3,64,4]{1,2,0:T(4,128)(2,1)S(1)}, u32[]{:S(2)}, u32[]{:S(2)}) collective-permute-start(bf16[3,64,4]{1,2,0:T(4,128)(2,1)S(1)} %copy-done.9), channel_id=1, source_target_pairs={{0,64},{64,128},{128,192},{192,0},{1,65},{65,129},{129,193},{193,1... | collective-permute-start | bytes 4616 | tf_op jit(solution)/shard_map/ppermute | solution.py:19
  38.8 43.9 %copy-start.2 = (bf16[3,8,4,4,576]{4,3,2,1,0:T(4,128)(2,1)}, bf16[3,8,4,4,576]{4,3,2,1,0:T(4,128)(2,1)S(1)}, u32[]{:S(2)}) copy-start(bf16[3,8,4,4,576]{4,3,2,1,0:T(4,128)(2,1)S(1)} %reshape.194) | copy-start | bytes 1327108
  43.3 7.3 %all-to-all-start.1 = ((bf16[4,2,256]{2,1,0:T(2,128)(2,1)}), bf16[4,2,256]{2,1,0:T(2,128)(2,1)S(1)}, u32[]{:S(2)}, u32[]{:S(2)}) async-start(bf16[4,2,256]{2,1,0:T(2,128)(2,1)} %reshape.281), calls=%async_computation.1 | async-start | bytes 8192 | tf_op jit(solution)/shard_map/all_to_all | solution.py:102
  46.5 214.1 %all-reduce.6.cloned.1.call-start = ((), (), s32[]{:S(2)}) async-start(), calls=%async_computation.5 | async-start | bytes 5505024 | tf_op jit(solution)/shard_map/psum | solution.py:169
  90.0 10.2 %slice-start = ((bf16[3,8,4,4,576]{4,3,2,1,0:T(4,128)(2,1)}), bf16[3,8,4,4,64]{4,3,2,1,0:T(4,128)(2,1)S(1)}, s32[]{:S(2)}) async-start(bf16[3,8,4,4,576]{4,3,2,1,0:T(4,128)(2,1)} %copy-done.2), calls=%async_computation.6 | async-start | bytes 196608 | tf_op jit(solution)/shard_map/slice | solution.py:133
  125.2 5.0 %copy-start.1 = (f32[3,1024,8,4,4]{1,2,4,3,0:T(8,128)S(1)}, f32[3,1024,8,4,4]{1,2,4,3,0:T(8,128)}, u32[]{:S(2)}) copy-start(f32[3,1024,8,4,4]{1,2,4,3,0:T(8,128)} %fusion.33) | copy-start | bytes 4718596
  125.2 5.0 %slice-start.1 = ((bf16[3,8,4,4,576]{4,3,2,1,0:T(4,128)(2,1)}), bf16[3,8,4,4,512]{4,3,2,1,0:T(4,128)(2,1)S(1)}, s32[]{:S(2)}) async-start(bf16[3,8,4,4,576]{4,3,2,1,0:T(4,128)(2,1)} %copy-done.2), calls=%async_computation.7 | async-start | bytes 786432 | tf_op jit(solution)/shard_map/slice | solution.py:130
  146.3 0.7 copy-start.7
  146.3 0.8 copy-start.10
  260.7 2.6 copy-start
  263.3 50.9 %copy-start.6 = (s32[3,8]{1,0:T(4,128)S(1)}, s32[3,8]{1,0:T(4,128)}, u32[]{:S(2)}) copy-start(s32[3,8]{1,0:T(4,128)} %param.21) | copy-start | bytes 292
Sparse Core Ops, SparseCore 0:
  20.9 41.4 all-gather.7
  64.2 55.1 all-gather.5
  146.4 114.2 all-reduce.5
where the time goes:
time: 324 us; the launch traced here: 321 us
  waiting for transfers between devices  140 us (43%)
  blocking collectives  96 us (30%)
  local copies, waits for them, and re-layouts  33 us (10%)
  matrix products  20.8 us (6%)
  between operations  14 us (4%)
  other arithmetic  11.9 us (4%)
  starting transfers between devices  5.67 us (2%)
    psum x1, waiting for transfers between devices, per_device(): lax.psum(jnp.dot(flat_values, w_out, preferred_element_type=jnp.float32),...  113 us
    unnamed x1, blocking collectives  45.7 us
    all_gather x1, blocking collectives, per_device(): lax.all_gather(incoming[2], 'tp', axis=1, tiled=True)  31.9 us
    all_gather x1, waiting for transfers between devices, per_device(): lax.all_gather(incoming[0], 'tp', axis=1, tiled=True)  17.5 us
    mul x2, local copies, waits for them, and re-layouts, per_device(): latent.reshape(requests, context, KVR // BLK, BLK).astype(jnp.float32)  13.4 us
    all_to_all x1, blocking collectives, per_device(): lax.all_to_all(outgoing[0], 'grp', split_axis=0, concat_axis=0, tiled=True)  10 us
    all_to_all x1, blocking collectives, per_device(): lax.all_to_all(outgoing[1], 'grp', split_axis=0, concat_axis=0, tiled=True)  8.4 us
    ppermute x3, waiting for transfers between devices, from_behind(): return lax.ppermute(value, axis, pairs)  7.57 us
  transfers between devices with their start and end apart: 7, of which 5 were waited for; matrix products, arithmetic and copies ran while one was open for 9% of the time, Pallas kernels for 0%

commit v1 on v0

v1 whole, which is shorter than its diff:
```python
import functools

import jax
import jax.numpy as jnp
from jax import lax
from jax.experimental import pallas as pl
from jax.experimental.pallas import tpu as pltpu
from jax.sharding import PartitionSpec as P

MESH = pl.DeviceIdType.MESH
BF16, F32 = jnp.bfloat16, jnp.float32

softmax_scale = 192.0 ** (-0.5)
norm_epsilon = 1e-06

NS, NG, NZ, NT = 4, 4, 8, 16
REQ, CAND, STEPS, HEADS = 3, 8, 4, 4
KVR, ROPE, KEY = 512, 64, 576
ROWS = REQ * CAND * STEPS
QROWS = HEADS * CAND * STEPS
D, HALF = 7168, 3584
BR, BC = 48, 896
HOP_A, HOP_B = 4, 3
PACK = 1152
VOCAB_LOCAL = 256


def nt_dot(a, b):
    return lax.dot_general(a, b, (((1,), (1,)), ((), ())), preferred_element_type=F32)


def nn_dot(a, b):
    return lax.dot_general(a, b, (((1,), (0,)), ((), ())), preferred_element_type=F32)


def unpack_key(slab, index):
    n = slab.shape[0]
    low = lax.broadcasted_iota(jnp.int32, (n, 128), 1) < ROPE
    start = index * KEY
    first = start // 128
    if index % 2 == 0:
        latent = slab[:, start : start + KVR]
        tile = slab[:, start + KVR : start + KVR + 128]
        rope_low = jnp.where(low, tile, 0.0)
        rope_high = pltpu.roll(rope_low, 64, 1)
    else:
        turned = [
            pltpu.roll(slab[:, (first + j) * 128 : (first + j + 1) * 128], 64, 1) for j in range(5)
        ]
        latent = jnp.concatenate([jnp.where(low, turned[j], turned[j + 1]) for j in range(4)], axis=1)
        rope_low = jnp.where(low, turned[4], 0.0)
        rope_high = pltpu.roll(rope_low, 64, 1)
    return latent, rope_low, rope_high


def kernel(
    dest, ctx_len, reply_len, lat_ref, rope_ref, scale_ref, reply_ref, target_ref,
    query_hbm, uv_hbm, out_hbm, vocab_hbm,
    score_ref,
    xsrc, sbuf, rbuf_0, rbuf_1, ctx, q_in, qn, qr, rkn, rkr, m_s, l_s, acc_s, att, hvbuf, wuv, wout, wvoc,
    snd_a, snd_b, rcv_a, rcv_b, hid, lg, ss, stat,
    local_sem, route_send, route_recv, ctx_send, ctx_recv, w_send, w_recv, hv_send, hv_recv,
    ra_send, ra_recv, rb_send, rb_recv, h_send, h_recv, st_send, st_recv,
):
    s, g, t = lax.axis_index("section"), lax.axis_index("grp"), lax.axis_index("tp")
    z, c = t // 2, t % 2
    sib = t + 1 - 2 * c
    sgn = 1 - 2 * c
    rbuf = (rbuf_0, rbuf_1)
    next_s = lax.rem(s + 1, NS)
    prev_s = lax.rem(s + NS - 1, NS)

    def ring(step):
        return lax.rem(z + sgn * step + 2 * NZ, NZ)

    dev_a = {"tp": ring(1) * 2 + c}
    dev_b = {"tp": ring(-1) * 2 + c}
    dev_sib = {"tp": sib}

    barrier = pltpu.get_barrier_semaphore()
    for k in range(NG):
        pl.semaphore_signal(barrier, inc=1, device_id={"section": next_s, "grp": k}, device_id_type=MESH)
        pl.semaphore_signal(barrier, inc=1, device_id={"section": prev_s, "grp": k}, device_id_type=MESH)
    for d in range(1, NT):
        pl.semaphore_signal(barrier, inc=1, device_id={"tp": lax.rem(t + d, NT)}, device_id_type=MESH)

    own_cols = pl.ds(pl.multiple_of(c * HALF, 128), HALF)
    other_cols = pl.ds(pl.multiple_of((1 - c) * HALF, 128), HALF)
    local = [
        pltpu.make_async_copy(query_hbm, q_in, local_sem.at[0]),
        pltpu.make_async_copy(uv_hbm, wuv, local_sem.at[1]),
        pltpu.make_async_copy(out_hbm.at[:, own_cols], wout.at[c], local_sem.at[2]),
        pltpu.make_async_copy(vocab_hbm, wvoc, local_sem.at[3]),
    ]
    local[0].start()

    row = lax.broadcasted_iota(jnp.int32, (64, 64), 0)
    col = lax.broadcasted_iota(jnp.int32, (64, 64), 1)
    place = 2 * ((row // 32) * 16 + row % 16) + (row // 16) % 2
    perm = (col == place).astype(BF16)
    for j in range(REQ):
        scale = scale_ref[j].astype(F32)
        parts = [
            (lat_ref[j, :, b * 128 : (b + 1) * 128].astype(F32) * scale[:, b : b + 1]).astype(BF16)
            for b in range(4)
        ]
        moved = nn_dot(perm, jnp.concatenate(parts, axis=1)).astype(BF16)
        for h in range(2):
            xsrc[j, h, :, 0:KVR] = moved[h * 32 : h * 32 + 16]
            xsrc[j, h, :, KVR : 2 * KVR] = moved[h * 32 + 16 : h * 32 + 32]
            xsrc[j, h, :, 2 * KVR : PACK] = rope_ref[j, h * 16 : (h + 1) * 16, :]

    own_dest = [dest[(s * NG + g) * REQ + j] for j in range(REQ)]
    for h in range(2):
        for k in range(NG):
            first = jnp.where(own_dest[0] == k, 0, jnp.where(own_dest[1] == k, 1, 2))
            last = jnp.where(own_dest[2] == k, 2, jnp.where(own_dest[1] == k, 1, 0))
            sbuf[h, k, 0] = xsrc[first, h]
            sbuf[h, k, 1] = xsrc[last, h]

    pl.semaphore_wait(barrier, 2 * NG + NT - 1)

    def route(h, k):
        return pltpu.make_async_remote_copy(
            src_ref=sbuf.at[h, k], dst_ref=rbuf[h].at[pl.ds(2 * g, 2)],
            send_sem=route_send.at[h, k], recv_sem=route_recv.at[h, g],
            device_id={"section": next_s, "grp": k}, device_id_type=MESH,
        )

    def route_arrived(h, k):
        return pltpu.make_async_remote_copy(
            src_ref=sbuf.at[h, k], dst_ref=rbuf[h].at[pl.ds(2 * k, 2)],
            send_sem=route_send.at[h, k], recv_sem=route_recv.at[h, k],
            device_id={"section": next_s, "grp": k}, device_id_type=MESH,
        )

    for h in range(2):
        for k in range(NG):
            route(h, k).start()
    w_copy = pltpu.make_async_remote_copy(
        src_ref=out_hbm.at[:, other_cols], dst_ref=wout.at[c],
        send_sem=w_send, recv_sem=w_recv, device_id=dev_sib, device_id_type=MESH,
    )
    w_arrive = pltpu.make_async_remote_copy(
        src_ref=out_hbm.at[:, other_cols], dst_ref=wout.at[1 - c],
        send_sem=w_send, recv_sem=w_recv, device_id=dev_sib, device_id_type=MESH,
    )
    w_copy.start()
    for copy in local[1:]:
        copy.start()

    picks = [jnp.int32(0)] * REQ
    count = jnp.int32(0)
    for h in range(NG):
        seen = jnp.int32(0)
        for j in range(REQ):
            hit = dest[(prev_s * NG + h) * REQ + j] == g
            for k in range(REQ):
                picks[k] = jnp.where(jnp.logical_and(hit, count == k), h * 2 + seen, picks[k])
            one = jnp.where(hit, 1, 0)
            seen = seen + one
            count = count + one
    picks = [jnp.minimum(pick, 2 * NG - 1) for pick in picks]

    local[0].wait()
    a_row = (lax.broadcasted_iota(jnp.int32, (QROWS, 32), 0) % 32) // STEPS
    t_row = lax.broadcasted_iota(jnp.int32, (QROWS, 32), 0) % STEPS
    a_col = lax.broadcasted_iota(jnp.int32, (QROWS, 32), 1) % CAND
    u_col = lax.broadcasted_iota(jnp.int32, (QROWS, 32), 1) // CAND
    reply_seen = jnp.logical_and(a_row == a_col, u_col <= t_row)

    def prepare(k, carry):
        slab = q_in[k].astype(F32)
        for h in range(HEADS):
            latent, low, high = unpack_key(slab, h)
            qn[k, h * 32 : (h + 1) * 32, :] = latent.astype(BF16)
            qr[k, h * 32 : (h + 1) * 32, :] = low.astype(BF16)
            qr[k, QROWS + h * 32 : QROWS + (h + 1) * 32, :] = high.astype(BF16)
        keys = reply_ref[k].astype(F32)
        pieces = [unpack_key(keys, u) for u in range(STEPS)]
        rkn[...] = jnp.concatenate([piece[0] for piece in pieces], axis=0).astype(BF16)
        rkr[...] = jnp.concatenate([piece[1] for piece in pieces], axis=0).astype(BF16)
        scores = nt_dot(qn[k], rkn[...]) + nt_dot(qr[k, 0:QROWS], rkr[...])
        scores = jnp.where(reply_seen, scores * softmax_scale, -jnp.inf)
        top = jnp.max(scores, axis=1, keepdims=True)
        weight = jnp.exp(scores - top)
        m_s[k] = top
        l_s[k] = jnp.sum(weight, axis=1, keepdims=True)
        acc_s[k] = nn_dot(weight.astype(BF16), rkn[...])
        return carry

    lax.fori_loop(0, REQ, prepare, 0)

    def ctx_copy(h, k, slot, way, device):
        return pltpu.make_async_remote_copy(
            src_ref=ctx.at[h, k, slot], dst_ref=ctx.at[h, k, slot],
            send_sem=ctx_send.at[h, k, slot, way], recv_sem=ctx_recv.at[h, k, slot],
            device_id=device, device_id_type=MESH,
        )

    def open_half(h):
        for k in range(NG):
            route_arrived(h, k).wait_recv()
        for k in range(REQ):
            ctx[h, k, t] = rbuf[h][picks[k]]
            ctx_copy(h, k, t, 0, dev_a).start()
            ctx_copy(h, k, t, 1, dev_b).start()
            ctx_copy(h, k, t, 2, dev_sib).start()

    def hop(h, i):
        def one(k, carry):
            slot = ring(-i) * 2 + c
            ctx_copy(h, k, slot, 0, dev_a).wait_recv()

            @pl.when(i < HOP_A)
            def _():
                ctx_copy(h, k, slot, 0, dev_a).start()

            ctx_copy(h, k, slot, 2, dev_sib).start()

            @pl.when(i <= HOP_B)
            def _():
                slot_b = ring(i) * 2 + c
                ctx_copy(h, k, slot_b, 1, dev_b).wait_recv()

                @pl.when(i < HOP_B)
                def _():
                    ctx_copy(h, k, slot_b, 1, dev_b).start()

                ctx_copy(h, k, slot_b, 2, dev_sib).start()

            return carry

        lax.fori_loop(0, REQ, one, 0)

    def from_sibling(h, k):
        def one(zz, carry):
            ctx_copy(h, k, zz * 2 + 1 - c, 2, dev_sib).wait_recv()
            return carry

        lax.fori_loop(0, NZ, one, 0)

    n_col = lax.broadcasted_iota(jnp.int32, (QROWS, 256), 1)
    n_pos = (n_col // 16) * 64 + 2 * (n_col % 16)

    def attend(h, k):
        even = ctx[h, k, :, :, 0:KVR].reshape(256, KVR)
        odd = ctx[h, k, :, :, KVR : 2 * KVR].reshape(256, KVR)
        rope = ctx[h, k, :, :, 2 * KVR : PACK].reshape(256, 128)
        query = qn[k]
        rope_scores = nt_dot(qr[k], rope)
        length = ctx_len[k]
        pos = n_pos + h * 32
        s_even = (nt_dot(query, even) + rope_scores[:QROWS]) * softmax_scale
        s_odd = (nt_dot(query, odd) + rope_scores[QROWS:]) * softmax_scale
        s_even = jnp.where(pos < length, s_even, -jnp.inf)
        s_odd = jnp.where(pos + 1 < length, s_odd, -jnp.inf)
        old = m_s[k]
        top = jnp.maximum(old, jnp.max(jnp.maximum(s_even, s_odd), axis=1, keepdims=True))
        fade = jnp.exp(old - top)
        p_even = jnp.exp(s_even - top)
        p_odd = jnp.exp(s_odd - top)
        m_s[k] = top
        l_s[k] = l_s[k] * fade + jnp.sum(p_even + p_odd, axis=1, keepdims=True)
        acc_s[k] = acc_s[k] * fade + (nn_dot(p_even.astype(BF16), even) + nn_dot(p_odd.astype(BF16), odd))

    open_half(0)
    for i in range(1, HOP_A + 1):
        hop(0, i)
        if i == 2:
            open_half(1)
    for i in range(1, HOP_A + 1):
        hop(1, i)
        if i < HOP_A:
            from_sibling(0, i - 1)
            attend(0, i - 1)

    def finish(k, carry):
        from_sibling(1, k)
        attend(1, k)
        rows = (acc_s[k] / l_s[k]).astype(BF16)
        at = pl.ds(pl.multiple_of(k * 32, 32), 32)
        for h in range(HEADS):
            att[h, at, :] = rows[h * 32 : (h + 1) * 32]
        return carry

    lax.fori_loop(0, REQ, finish, 0)

    local[1].wait()
    for h in range(HEADS):
        hvbuf[c, :, h * 128 : (h + 1) * 128] = nn_dot(att[h], wuv[:, h * 128 : (h + 1) * 128]).astype(BF16)
    hv_copy = pltpu.make_async_remote_copy(
        src_ref=hvbuf.at[c], dst_ref=hvbuf.at[c], send_sem=hv_send, recv_sem=hv_recv,
        device_id=dev_sib, device_id_type=MESH,
    )
    hv_arrive = pltpu.make_async_remote_copy(
        src_ref=hvbuf.at[1 - c], dst_ref=hvbuf.at[1 - c], send_sem=hv_send, recv_sem=hv_recv,
        device_id=dev_sib, device_id_type=MESH,
    )
    hv_copy.start()
    local[2].wait()
    w_arrive.wait_recv()
    hv_arrive.wait_recv()

    def block_rows(zb):
        return pl.ds(pl.multiple_of((zb % 2) * BR, 16), BR)

    def partial(zb):
        rows = block_rows(zb)
        cols = pl.ds(pl.multiple_of((zb // 2) * BC, 128), BC)
        return nn_dot(hvbuf[0, rows, :], wout[0, :, cols]) + nn_dot(hvbuf[1, rows, :], wout[1, :, cols])

    def push_a(i):
        return pltpu.make_async_remote_copy(
            src_ref=snd_a.at[i], dst_ref=rcv_a.at[i], send_sem=ra_send.at[i], recv_sem=ra_recv.at[i],
            device_id=dev_a, device_id_type=MESH,
        )

    def push_b(i):
        return pltpu.make_async_remote_copy(
            src_ref=snd_b.at[i], dst_ref=rcv_b.at[i], send_sem=rb_send.at[i], recv_sem=rb_recv.at[i],
            device_id=dev_b, device_id_type=MESH,
        )

    snd_a[0] = partial(ring(HOP_A)).astype(BF16)
    push_a(0).start()
    snd_b[0] = partial(ring(-HOP_B)).astype(BF16)
    push_b(0).start()

    def reduce_step(i, carry):
        term = partial(ring(HOP_A - i))
        push_a(i - 1).wait_recv()
        snd_a[i] = (term + rcv_a[i - 1].astype(F32)).astype(BF16)
        push_a(i).start()

        @pl.when(i < HOP_B)
        def _():
            term_b = partial(ring(i - HOP_B))
            push_b(i - 1).wait_recv()
            snd_b[i] = (term_b + rcv_b[i - 1].astype(F32)).astype(BF16)
            push_b(i).start()

        return carry

    lax.fori_loop(1, HOP_A, reduce_step, 0)
    own = partial(z)
    push_b(HOP_B - 1).wait_recv()
    own = own + rcv_b[HOP_B - 1].astype(F32)
    push_a(HOP_A - 1).wait_recv()
    own = own + rcv_a[HOP_A - 1].astype(F32)

    def hid_copy(zb, way, device):
        return pltpu.make_async_remote_copy(
            src_ref=hid.at[c, zb], dst_ref=hid.at[c, zb], send_sem=h_send.at[zb, way],
            recv_sem=h_recv.at[c, zb], device_id=device, device_id_type=MESH,
        )

    def hid_sibling(zb):
        return pltpu.make_async_remote_copy(
            src_ref=hid.at[1 - c, zb], dst_ref=hid.at[1 - c, zb], send_sem=h_send.at[zb, 2],
            recv_sem=h_recv.at[1 - c, zb], device_id=dev_sib, device_id_type=MESH,
        )

    lg[...] = jnp.zeros_like(lg)
    ss[...] = jnp.zeros_like(ss)

    def use(core, zb):
        rows = block_rows(zb)
        x = hid[core, zb]
        depth = pl.ds(pl.multiple_of(core * HALF + (zb // 2) * BC, 128), BC)
        lg[rows, :] += nn_dot(x, wvoc[depth, :])
        wide = x.astype(F32)
        square = wide * wide
        total = square[:, 0:128]
        for j in range(1, BC // 128):
            total = total + square[:, j * 128 : (j + 1) * 128]
        ss[rows, :] += total

    hid[c, z] = own.astype(BF16)
    hid_copy(z, 0, dev_a).start()
    hid_copy(z, 1, dev_b).start()
    hid_copy(z, 2, dev_sib).start()
    local[3].wait()
    use(c, z)

    def gather_step(i, carry):
        za = ring(-i)
        hid_copy(za, 0, dev_a).wait_recv()

        @pl.when(i < HOP_A)
        def _():
            hid_copy(za, 0, dev_a).start()

        hid_copy(za, 2, dev_sib).start()

        @pl.when(i <= HOP_B)
        def _():
            zb = ring(i)
            hid_copy(zb, 1, dev_b).wait_recv()

            @pl.when(i < HOP_B)
            def _():
                hid_copy(zb, 1, dev_b).start()

            hid_copy(zb, 2, dev_sib).start()
            use(c, zb)

        use(c, za)
        back = ring(i - 1)
        hid_sibling(back).wait_recv()
        use(1 - c, back)

        @pl.when(i > 1)
        def _():
            ahead = ring(1 - i)
            hid_sibling(ahead).wait_recv()
            use(1 - c, ahead)

        return carry

    lax.fori_loop(1, HOP_A + 1, gather_step, 0)
    last = ring(HOP_A)
    hid_sibling(last).wait_recv()
    use(1 - c, last)

    lane = lax.broadcasted_iota(jnp.int32, (ROWS, 128), 1)
    wide_targets = jnp.concatenate(
        [target_ref[...].astype(F32), jnp.zeros((REQ, 96), F32)], axis=1
    )
    wide_targets = jnp.concatenate([wide_targets, jnp.zeros((8 - REQ, 128), F32)], axis=0)
    turned = jnp.transpose(jnp.concatenate([wide_targets] * 16, axis=0))
    target_col = jnp.concatenate([turned[0:32, k : k + 1] for k in range(REQ)], axis=0).astype(jnp.int32)
    factor = lax.rsqrt(jnp.sum(ss[...], axis=1, keepdims=True) * (1.0 / D) + norm_epsilon)
    logits = lg[...] * factor
    top = jnp.max(logits, axis=1, keepdims=True)
    total = jnp.sum(jnp.exp(logits - top), axis=1, keepdims=True)
    hit = lax.broadcasted_iota(jnp.int32, (ROWS, VOCAB_LOCAL), 1) == target_col - t * VOCAB_LOCAL
    aimed = jnp.sum(jnp.where(hit, logits, 0.0), axis=1, keepdims=True)
    table = jnp.where(lane == 0, top, jnp.where(lane == 1, total, jnp.where(lane == 2, aimed, 0.0)))
    table = jnp.concatenate([table, jnp.zeros((128 - ROWS, 128), F32)], axis=0)
    stat[t] = jnp.transpose(table)[0:8, :]

    def stat_copy(d):
        return pltpu.make_async_remote_copy(
            src_ref=stat.at[t], dst_ref=stat.at[t], send_sem=st_send.at[d], recv_sem=st_recv.at[t],
            device_id={"tp": lax.rem(t + d, NT)}, device_id_type=MESH,
        )

    def stat_arrive(d):
        peer = lax.rem(t + d, NT)
        return pltpu.make_async_remote_copy(
            src_ref=stat.at[peer], dst_ref=stat.at[peer], send_sem=st_send.at[d], recv_sem=st_recv.at[peer],
            device_id={"tp": peer}, device_id_type=MESH,
        )

    for d in range(1, NT):
        stat_copy(d).start()

    def drain_ctx(index, carry):
        h, k = index // REQ, index % REQ
        for i in range(HOP_A):
            ctx_copy(h, k, ring(-i) * 2 + c, 0, dev_a).wait_send()
        for i in range(HOP_B):
            ctx_copy(h, k, ring(i) * 2 + c, 1, dev_b).wait_send()
        for zz in range(NZ):
            ctx_copy(h, k, zz * 2 + c, 2, dev_sib).wait_send()
        return carry

    lax.fori_loop(0, 2 * REQ, drain_ctx, 0)
    for h in range(2):
        for k in range(NG):
            route(h, k).wait_send()
    w_copy.wait_send()
    hv_copy.wait_send()
    for i in range(HOP_A):
        push_a(i).wait_send()
        hid_copy(ring(-i), 0, dev_a).wait_send()
    for i in range(HOP_B):
        push_b(i).wait_send()
        hid_copy(ring(i), 1, dev_b).wait_send()
    for zz in range(NZ):
        hid_copy(zz, 2, dev_sib).wait_send()

    lane1 = lax.broadcasted_iota(jnp.int32, (1, 128), 1)
    length = jnp.ones((1, 128), jnp.int32)
    for k in range(REQ):
        for a in range(CAND):
            length = jnp.where(lane1 // STEPS == k * CAND + a, reply_len[k, a], length)

    for d in range(1, NT):
        stat_arrive(d).wait_recv()
    every = [stat[d] for d in range(NT)]
    joint = functools.reduce(jnp.maximum, [one[0:1] for one in every])
    joint_total = functools.reduce(jnp.add, [one[1:2] * jnp.exp(one[0:1] - joint) for one in every])
    joint_aimed = functools.reduce(jnp.add, [one[2:3] for one in every])
    log_prob = joint_aimed - (joint + jnp.log(joint_total))
    inside = jnp.logical_and(lane1 % STEPS < length, lane1 < ROWS)
    value = jnp.where(inside, log_prob, 0.0) / length.astype(F32)
    spread = jnp.where(
        lax.broadcasted_iota(jnp.int32, (8, 128), 1) // 32 == lax.broadcasted_iota(jnp.int32, (8, 128), 0),
        jnp.broadcast_to(value, (8, 128)),
        0.0,
    )
    source_lane = lax.broadcasted_iota(jnp.int32, (128, 128), 0)
    pick = ((source_lane % 32) // STEPS == lax.broadcasted_iota(jnp.int32, (128, 128), 1)).astype(F32)
    summed = lax.dot_general(
        spread, pick, (((1,), (0,)), ((), ())), precision=lax.Precision.HIGHEST, preferred_element_type=F32
    )
    score_ref[...] = summed[0:REQ, 0:CAND]
    for d in range(1, NT):
        stat_copy(d).wait_send()


def per_device(
    ctx_latent, ctx_rope, ctx_scale, dest, ctx_len, queries, reply_keys, reply_len, targets, w_uv, w_out, w_vocab
):
    vmem = pl.BlockSpec(memory_space=pltpu.VMEM)
    smem = pl.BlockSpec(memory_space=pltpu.SMEM)
    hbm = pl.BlockSpec(memory_space=pl.ANY)
    dma = pltpu.SemaphoreType.DMA
    return pl.pallas_call(
        kernel,
        out_shape=jax.ShapeDtypeStruct((REQ, CAND), F32),
        in_specs=[smem, smem, smem, vmem, vmem, vmem, vmem, vmem, hbm, hbm, hbm, hbm],
        out_specs=vmem,
        scratch_shapes=[
            pltpu.VMEM((REQ, 2, 16, PACK), BF16),
            pltpu.VMEM((2, NG, 2, 16, PACK), BF16),
            pltpu.VMEM((NG * 2, 16, PACK), BF16),
            pltpu.VMEM((NG * 2, 16, PACK), BF16),
            pltpu.VMEM((2, REQ, NT, 16, PACK), BF16),
            pltpu.VMEM((REQ, 32, HEADS * KEY), BF16),
            pltpu.VMEM((REQ, QROWS, KVR), BF16),
            pltpu.VMEM((REQ, 2 * QROWS, 128), BF16),
            pltpu.VMEM((32, KVR), BF16),
            pltpu.VMEM((32, 128), BF16),
            pltpu.VMEM((REQ, QROWS, 1), F32),
            pltpu.VMEM((REQ, QROWS, 1), F32),
            pltpu.VMEM((REQ, QROWS, KVR), F32),
            pltpu.VMEM((HEADS, ROWS, KVR), BF16),
            pltpu.VMEM((2, ROWS, 512), BF16),
            pltpu.VMEM((KVR, 512), BF16),
            pltpu.VMEM((2, 512, HALF), BF16),
            pltpu.VMEM((D, VOCAB_LOCAL), BF16),
            pltpu.VMEM((HOP_A, BR, BC), BF16),
            pltpu.VMEM((HOP_B, BR, BC), BF16),
            pltpu.VMEM((HOP_A, BR, BC), BF16),
            pltpu.VMEM((HOP_B, BR, BC), BF16),
            pltpu.VMEM((2, NZ, BR, BC), BF16),
            pltpu.VMEM((ROWS, VOCAB_LOCAL), F32),
            pltpu.VMEM((ROWS, 128), F32),
            pltpu.VMEM((NT, 8, 128), F32),
            dma((4,)),
            dma((2, NG)),
            dma((2, NG)),
            dma((2, REQ, NT, 3)),
            dma((2, REQ, NT)),
            dma, dma, dma, dma,
            dma((HOP_A,)), dma((HOP_A,)), dma((HOP_B,)), dma((HOP_B,)),
            dma((NZ, 3)), dma((2, NZ)),
            dma((NT,)), dma((NT,)),
        ],
        compiler_params=pltpu.CompilerParams(
            collective_id=0, has_side_effects=True, vmem_limit_bytes=48 * 1024 * 1024
        ),
    )(
        dest, ctx_len, reply_len, ctx_latent, ctx_rope, ctx_scale, reply_keys, targets,
        queries, w_uv, w_out, w_vocab,
    )


def solution(mesh):
    group = ("section", "grp")
    placed = (
        P(group, "tp", None),
        P(group, "tp", None),
        P(group, "tp", None),
        P(),
        P(group),
        P(group, None, "tp"),
        P(group, None, None),
        P(group, None),
        P(group, None),
        P(None, "tp"),
        P("tp", None),
        P(None, "tp"),
    )
    return jax.shard_map(
        per_device, mesh=mesh, in_specs=placed, out_specs=P(group, None), check_vma=False
    )
```

time: 324 us -> 109 us (0.34)
  waiting for transfers between devices: 140 us -> 0 us
  Pallas kernels: 0 us -> 97.4 us
  blocking collectives: 96 us -> 0 us
  local copies, waits for them, and re-layouts: 33 us -> 10.7 us
  matrix products: 20.8 us -> 0 us
  between operations: 14 us -> 0.03 us
  other arithmetic: 11.9 us -> 0 us
  starting transfers between devices: 5.67 us -> 0 us
    psum x1 -> x0, waiting for transfers between devices: 113 us -> none  [per_device(): lax.psum(jnp.dot(flat_values, w_out, preferred_element_type=jnp.float32),...]
    pallas_call x0 -> x1, Pallas kernels: none -> 97.4 us  [per_device(): pl.pallas_call(kernel, out_shape=jax.ShapeDtypeStruct((REQ, CAND), F32),...]
    unnamed x1 -> x0, blocking collectives: 45.7 us -> none
    all_gather x1 -> x0, blocking collectives: 31.9 us -> none  [per_device(): lax.all_gather(incoming[2], 'tp', axis=1, tiled=True)]
    dot_general x7 -> x0, matrix products: 20.8 us -> none  [the longest x1 5.95 us: per_device(): jnp.dot(flat_values, w_out, preferred_element_type=jnp.float32)]
    all_to_all x2 -> x0, blocking collectives: 18.4 us -> none  [the longest x1 10 us: per_device(): lax.all_to_all(outgoing[0], 'grp', split_axis=0, concat_axis=0, tiled=True)]
    all_gather x2 -> x0, waiting for transfers between devices: 17.5 us -> none  [the longest x1 17.5 us: per_device(): lax.all_gather(incoming[0], 'tp', axis=1, tiled=True)]
    mul x2 -> x0, local copies, waits for them, and re-layouts: 13.4 us -> none  [per_device(): latent.reshape(requests, context, KVR // BLK, BLK).astype(jnp.float32)]
  transfers between devices with their start and end apart: 7 -> 0, of which waited for: 5 -> 0; matrix products, arithmetic and copies ran while one was open for 9% -> 0% of each run, Pallas kernels for 0% -> 0%
where the time goes in v1:
time: 109 us; the launch traced here: 108 us
  Pallas kernels  97.4 us (89%)
  local copies, waits for them, and re-layouts  10.7 us (10%)
    pallas_call x1, Pallas kernels, per_device(): pl.pallas_call(kernel, out_shape=jax.ShapeDtypeStruct((REQ, CAND), F32),...  97.4 us
    unnamed x22, local copies, waits for them, and re-layouts  10.7 us

profile of v1, /device:TPU:1, one launch (start us, length us, event | category | flops | bytes accessed | tf_op | source)
XLA Modules:
  0.0 108.1 jit_solution(15150273944930086451)
XLA Ops:
  0.0 0.8 copy.13.scale_ref
  0.8 0.0 copy-start
  0.8 2.0 %copy-done = bf16[7168,256]{1,0:T(8,128)(2,1)S(1)} copy-done((bf16[7168,256]{1,0:T(8,128)(2,1)S(1)}, bf16[7168,256]{1,0:T(8,128)(2,1)}, u32[]{:S(2)}) %copy-start) | copy-done | bytes 3670040
  2.9 0.0 copy-start.1
  2.9 1.0 copy-done.1
  3.9 0.0 copy-start.2
  3.9 1.0 copy-done.2
  4.9 0.0 copy-start.3
  4.9 0.9 copy-done.3
  5.8 0.0 copy-start.4
  5.8 0.9 copy-done.4
  6.7 0.0 copy-start.5
  6.7 0.7 copy-done.5
  7.5 0.0 copy-start.6
  7.5 0.7 copy-done.6
  8.2 0.0 copy-start.7
  8.2 0.7 copy-done.7
  8.8 0.0 copy-start.8
  8.8 0.7 copy-done.8
  9.5 0.0 copy-start.9
  9.5 0.7 copy-done.9
  10.2 97.4 %shard_map.118 = f32[3,8]{1,0:T(4,128)S(1)} custom-call(s32[48]{0:T(128)S(1)} %copy-done.8, s32[3]{0:T(128)S(1)} %copy-done.9, s32[3,8]{1,0:T(4,128)S(1)} %copy-done.6, bf16[3,64,512]{2,1,0:T(8,128)(2,1)S(1)} %copy-done.3, bf16[3,32,128]{2,1,0:T(8,128)(2,1)S(1)} %copy-done.5, bf16[3,64,4]{2,1,0:T(8,128)(2,1)S(1)} %copy.13.scale_ref, ...), custom_call_target="tpu_custom_call" | custom-call | tf_op jit(solution)/shard_map/pallas_call | solution.py:521
  107.5 0.6 copy.15
Async XLA Ops:
  0.8 2.0 %copy-start = (bf16[7168,256]{1,0:T(8,128)(2,1)S(1)}, bf16[7168,256]{1,0:T(8,128)(2,1)}, u32[]{:S(2)}) copy-start(bf16[7168,256]{1,0:T(8,128)(2,1)} %vocab_hbm.1) | copy-start | bytes 11010052
  2.9 1.0 copy-start.1
  3.9 1.0 copy-start.2
  4.9 0.9 copy-start.3
  5.8 0.9 copy-start.4
  6.7 0.7 copy-start.5
  7.5 0.7 copy-start.6
  8.2 0.7 copy-start.7
  8.8 0.7 copy-start.8
  9.5 0.7 copy-start.9

commit v2 on v1

v2 whole, which is shorter than its diff:
```python
import functools

import jax
import jax.numpy as jnp
from jax import lax
from jax.experimental import pallas as pl
from jax.experimental.pallas import tpu as pltpu
from jax.sharding import PartitionSpec as P

MESH = pl.DeviceIdType.MESH
BF16, F32 = jnp.bfloat16, jnp.float32

softmax_scale = 192.0 ** (-0.5)
norm_epsilon = 1e-06

NS, NG, NZ, NT = 4, 4, 8, 16
REQ, CAND, STEPS, HEADS = 3, 8, 4, 4
KVR, ROPE, KEY = 512, 64, 576
ROWS = REQ * CAND * STEPS
QROWS = HEADS * CAND * STEPS
D, HALF = 7168, 3584
BR, BC = 48, 896
HOP_A, HOP_B = 4, 3
WIDE_A, WIDE_B = 640, 512
CHUNKS = 4
VOCAB_LOCAL = 256
ROUTE, USE = -1, -2
SCHEDULE = (
    (1, ROUTE), (0, 0), (2, ROUTE), (1, 0), (0, 1), (3, ROUTE), (2, 0), (1, 1), (0, 2), (3, 0), (2, 1), (1, 2), (0, 3),
    (3, 1), (2, 2), (1, 3), (0, 4), (3, 2), (2, 3), (1, 4), (0, USE), (3, 3), (2, 4), (1, USE), (3, 4), (2, USE), (3, USE),
)


def nt_dot(a, b):
    return lax.dot_general(a, b, (((1,), (1,)), ((), ())), preferred_element_type=F32)


def nn_dot(a, b):
    return lax.dot_general(a, b, (((1,), (0,)), ((), ())), preferred_element_type=F32)


def unpack_key(slab, index):
    n = slab.shape[0]
    low = lax.broadcasted_iota(jnp.int32, (n, 128), 1) < ROPE
    start = index * KEY
    first = start // 128
    if index % 2 == 0:
        latent = slab[:, start : start + KVR]
        tile = slab[:, start + KVR : start + KVR + 128]
        rope_low = jnp.where(low, tile, 0.0)
        rope_high = pltpu.roll(rope_low, 64, 1)
    else:
        turned = [
            pltpu.roll(slab[:, (first + j) * 128 : (first + j + 1) * 128], 64, 1) for j in range(5)
        ]
        latent = jnp.concatenate([jnp.where(low, turned[j], turned[j + 1]) for j in range(4)], axis=1)
        rope_low = jnp.where(low, turned[4], 0.0)
        rope_high = pltpu.roll(rope_low, 64, 1)
    return latent, rope_low, rope_high


def kernel(
    dest_hbm, ctx_len_hbm, reply_len_hbm, lat_hbm, rope_hbm, scale_hbm, reply_hbm, target_hbm,
    query_hbm, uv_hbm, out_hbm, vocab_hbm,
    score_ref,
    dest, ctx_len, reply_len, lat_ref, rope_ref, scale_ref, reply_ref, target_ref, xsrc_a, xsrc_b, sbuf_a, sbuf_b, rbuf_0, rbuf_1, rbuf_2, rbuf_3, ctx_a, ctx_b, q_in, qn, qr, rkn, rkr, m_s, l_s, acc_s, att, hvbuf, wuv, wout, wvoc,
    part, snd, rcv, hid, lg, ss, stat,
    local_sem, route_send, route_recv, ctx_send, ctx_recv, w_send, w_recv, hv_send, hv_recv,
    r_send, r_recv, h_send, h_recv, st_send, st_recv,
):
    s, g, t = lax.axis_index("section"), lax.axis_index("grp"), lax.axis_index("tp")
    z, c = t // 2, t % 2
    sib = t + 1 - 2 * c
    sgn = 1 - 2 * c
    xsrc, sbuf, ctx = (xsrc_a, xsrc_b), (sbuf_a, sbuf_b), (ctx_a, ctx_b)
    rbuf = (rbuf_0, rbuf_1, rbuf_2, rbuf_3)
    next_s = lax.rem(s + 1, NS)
    prev_s = lax.rem(s + NS - 1, NS)

    def ring(step):
        return lax.rem(z + sgn * step + 2 * NZ, NZ)

    dev_a, dev_b = {"tp": ring(1) * 2 + c}, {"tp": ring(-1) * 2 + c}
    dev_a2, dev_b2 = {"tp": ring(2) * 2 + c}, {"tp": ring(-2) * 2 + c}
    dev_sib = {"tp": sib}

    barrier = pltpu.get_barrier_semaphore()
    for k in range(NG):
        pl.semaphore_signal(barrier, inc=1, device_id={"section": prev_s, "grp": k}, device_id_type=MESH)
    for device in (dev_a, dev_b, dev_a2, dev_b2, dev_sib):
        pl.semaphore_signal(barrier, inc=1, device_id=device, device_id_type=MESH)

    own_cols = pl.ds(pl.multiple_of(c * HALF, 128), HALF)
    other_cols = pl.ds(pl.multiple_of((1 - c) * HALF, 128), HALF)
    pairs = [
        (scale_hbm, scale_ref), (lat_hbm, lat_ref), (rope_hbm, rope_ref), (dest_hbm, dest),
        (query_hbm, q_in), (reply_hbm, reply_ref), (ctx_len_hbm, ctx_len),
        (uv_hbm, wuv), (out_hbm.at[:, own_cols], wout.at[c]), (vocab_hbm, wvoc),
        (target_hbm, target_ref), (reply_len_hbm, reply_len),
    ]
    local = [pltpu.make_async_copy(a, b, local_sem.at[i]) for i, (a, b) in enumerate(pairs)]
    for copy in local:
        copy.start()

    row = lax.broadcasted_iota(jnp.int32, (64, 64), 0)
    col = lax.broadcasted_iota(jnp.int32, (64, 64), 1)
    place = 2 * ((row // 32) * 16 + row % 16) + (row // 16) % 2
    perm = (col == place).astype(BF16)
    for copy in local[:4]:
        copy.wait()
    scales = jnp.concatenate([scale_ref[j].astype(F32) for j in range(REQ)] + [jnp.zeros((4, 64), F32)], axis=0)
    scales = jnp.concatenate([scales, jnp.zeros((16, 64), F32)], axis=1)
    scales = jnp.transpose(jnp.concatenate([scales] * 8, axis=0))
    for j in range(REQ):
        parts = [
            (lat_ref[j, :, b * 128 : (b + 1) * 128].astype(F32) * scales[0:64, j * 4 + b : j * 4 + b + 1]).astype(BF16)
            for b in range(4)
        ]
        moved = nn_dot(perm, jnp.concatenate(parts, axis=1)).astype(BF16)
        for h in range(2):
            xsrc_a[j, h, :, 0:KVR] = moved[h * 32 : h * 32 + 16]
            xsrc_a[j, h, :, KVR:WIDE_A] = rope_ref[j, h * 16 : (h + 1) * 16, :]
            xsrc_b[j, h] = moved[h * 32 + 16 : h * 32 + 32]

    own_dest = [dest[(s * NG + g) * REQ + j] for j in range(REQ)]
    for h in range(CHUNKS):
        for k in range(NG):
            first = jnp.where(own_dest[0] == k, 0, jnp.where(own_dest[1] == k, 1, 2))
            last = jnp.where(own_dest[2] == k, 2, jnp.where(own_dest[1] == k, 1, 0))
            sbuf[h % 2][h // 2, k, 0] = xsrc[h % 2][first, h // 2]
            sbuf[h % 2][h // 2, k, 1] = xsrc[h % 2][last, h // 2]

    pl.semaphore_wait(barrier, NG + 5)

    def route(h, j):
        k = lax.rem(g + j, NG)
        return pltpu.make_async_remote_copy(
            src_ref=sbuf[h % 2].at[h // 2, k], dst_ref=rbuf[h].at[pl.ds(2 * g, 2)],
            send_sem=route_send.at[h, j], recv_sem=route_recv.at[h, g],
            device_id={"section": next_s, "grp": k}, device_id_type=MESH,
        )

    def route_arrived(h, k):
        return pltpu.make_async_remote_copy(
            src_ref=sbuf[h % 2].at[h // 2, k], dst_ref=rbuf[h].at[pl.ds(2 * k, 2)],
            send_sem=route_send.at[h, k], recv_sem=route_recv.at[h, k],
            device_id={"section": next_s, "grp": k}, device_id_type=MESH,
        )

    def route_start(h):
        for k in range(NG):
            route(h, k).start()

    def route_left(h):
        for k in range(NG):
            route(h, k).wait_send()

    route_start(0)
    w_copy = pltpu.make_async_remote_copy(
        src_ref=out_hbm.at[:, other_cols], dst_ref=wout.at[c],
        send_sem=w_send, recv_sem=w_recv, device_id=dev_sib, device_id_type=MESH,
    )
    w_arrive = pltpu.make_async_remote_copy(
        src_ref=out_hbm.at[:, other_cols], dst_ref=wout.at[1 - c],
        send_sem=w_send, recv_sem=w_recv, device_id=dev_sib, device_id_type=MESH,
    )

    def drain_route():
        route_left(CHUNKS - 1)
        w_copy.wait_send()

    picks = [jnp.int32(0)] * REQ
    count = jnp.int32(0)
    for h in range(NG):
        seen = jnp.int32(0)
        for j in range(REQ):
            hit = dest[(prev_s * NG + h) * REQ + j] == g
            for k in range(REQ):
                picks[k] = jnp.where(jnp.logical_and(hit, count == k), h * 2 + seen, picks[k])
            one = jnp.where(hit, 1, 0)
            seen = seen + one
            count = count + one
    picks = [jnp.minimum(pick, 2 * NG - 1) for pick in picks]

    for copy in local[4:7]:
        copy.wait()
    a_row = (lax.broadcasted_iota(jnp.int32, (QROWS, 32), 0) % 32) // STEPS
    t_row = lax.broadcasted_iota(jnp.int32, (QROWS, 32), 0) % STEPS
    a_col = lax.broadcasted_iota(jnp.int32, (QROWS, 32), 1) % CAND
    u_col = lax.broadcasted_iota(jnp.int32, (QROWS, 32), 1) // CAND
    reply_seen = jnp.logical_and(a_row == a_col, u_col <= t_row)

    def prepare(k, carry):
        slab = q_in[k].astype(F32)
        for h in range(HEADS):
            latent, low, high = unpack_key(slab, h)
            qn[k, h * 32 : (h + 1) * 32, :] = latent.astype(BF16)
            qr[k, h * 32 : (h + 1) * 32, :] = low.astype(BF16)
            qr[k, QROWS + h * 32 : QROWS + (h + 1) * 32, :] = high.astype(BF16)
        keys = reply_ref[k].astype(F32)
        pieces = [unpack_key(keys, u) for u in range(STEPS)]
        rkn[...] = jnp.concatenate([piece[0] for piece in pieces], axis=0).astype(BF16)
        rkr[...] = jnp.concatenate([piece[1] for piece in pieces], axis=0).astype(BF16)
        scores = nt_dot(qn[k], rkn[...]) + nt_dot(qr[k, 0:QROWS], rkr[...])
        scores = jnp.where(reply_seen, scores * softmax_scale, -jnp.inf)
        top = jnp.max(scores, axis=1, keepdims=True)
        weight = jnp.exp(scores - top)
        m_s[k] = top
        l_s[k] = jnp.sum(weight, axis=1, keepdims=True)
        acc_s[k] = nn_dot(weight.astype(BF16), rkn[...])
        return carry

    lax.fori_loop(0, REQ, prepare, 0)

    def ctx_copy(h, slot, way, device):
        block = ctx[h % 2].at[h // 2, slot]
        return pltpu.make_async_remote_copy(
            src_ref=block, dst_ref=block, send_sem=ctx_send.at[h, slot, way], recv_sem=ctx_recv.at[h, slot],
            device_id=device, device_id_type=MESH,
        )

    ctx_ways = (dev_a, dev_b, dev_sib)

    def open_chunk(h):
        for k in range(NG):
            route_arrived(h, k).wait_recv()
        for k in range(REQ):
            ctx[h % 2][h // 2, t, k] = rbuf[h][picks[k]]
        for way in range(3):
            ctx_copy(h, t, way, ctx_ways[way]).start()

    def share(h, slot, *onward):
        ctx_copy(h, slot, 0, dev_a).wait_recv()
        for way in onward:
            ctx_copy(h, slot, way, ctx_ways[way]).start()
        ctx_copy(h, slot, 2, dev_sib).start()

    def hop(h, i):
        share(h, ring(-i) * 2 + c, *((0,) if i < HOP_A else ()))
        if i <= HOP_B:
            share(h, ring(i) * 2 + c, *((1,) if i < HOP_B else ()))

    n_col = lax.broadcasted_iota(jnp.int32, (QROWS, 256), 1)
    n_pos = (n_col // 16) * 64 + 2 * (n_col % 16)

    def attend(h, k):
        if h % 2 == 0:
            latent = ctx_a[h // 2, :, k, :, 0:KVR].reshape(256, KVR)
            rope_query = qr[k, 0:QROWS]
        else:
            latent = ctx_b[h // 2, :, k].reshape(256, KVR)
            rope_query = qr[k, QROWS : 2 * QROWS]
        rope = ctx_a[h // 2, :, k, :, KVR:WIDE_A].reshape(256, 128)
        scores = (nt_dot(qn[k], latent) + nt_dot(rope_query, rope)) * softmax_scale
        scores = jnp.where(n_pos + (h // 2) * 32 + h % 2 < ctx_len[k], scores, -jnp.inf)
        old = m_s[k]
        top = jnp.maximum(old, jnp.max(scores, axis=1, keepdims=True))
        fade = jnp.exp(old - top)
        weight = jnp.exp(scores - top)
        m_s[k] = top
        l_s[k] = l_s[k] * fade + jnp.sum(weight, axis=1, keepdims=True)
        acc_s[k] = acc_s[k] * fade + nn_dot(weight.astype(BF16), latent)

    def close_chunk(h):
        def one(zz, carry):
            ctx_copy(h, zz * 2 + 1 - c, 2, dev_sib).wait_recv()
            return carry

        lax.fori_loop(0, NZ, one, 0)

    for h, i in SCHEDULE:
        if i == ROUTE:
            route_left(h - 1)
            route_start(h)
            if h == CHUNKS - 1:
                w_copy.start()
        elif i == USE:
            close_chunk(h)
            for k in range(REQ):
                attend(h, k)
        elif i == 0:
            open_chunk(h)
        else:
            hop(h, i)
    for k in range(REQ):
        rows = (acc_s[k] / l_s[k]).astype(BF16)
        for h in range(HEADS):
            att[h, k * 32 : (k + 1) * 32, :] = rows[h * 32 : (h + 1) * 32]

    def drain_ctx():
        for h in range(CHUNKS):
            for i in range(HOP_A):
                ctx_copy(h, ring(-i) * 2 + c, 0, dev_a).wait_send()
            for i in range(HOP_B):
                ctx_copy(h, ring(i) * 2 + c, 1, dev_b).wait_send()
            for zz in range(NZ):
                ctx_copy(h, zz * 2 + c, 2, dev_sib).wait_send()

    local[7].wait()
    for h in range(HEADS):
        hvbuf[c, :, h * 128 : (h + 1) * 128] = nn_dot(att[h], wuv[:, h * 128 : (h + 1) * 128]).astype(BF16)
    hv_copy = pltpu.make_async_remote_copy(
        src_ref=hvbuf.at[c], dst_ref=hvbuf.at[c], send_sem=hv_send, recv_sem=hv_recv,
        device_id=dev_sib, device_id_type=MESH,
    )
    hv_arrive = pltpu.make_async_remote_copy(
        src_ref=hvbuf.at[1 - c], dst_ref=hvbuf.at[1 - c], send_sem=hv_send, recv_sem=hv_recv,
        device_id=dev_sib, device_id_type=MESH,
    )
    hv_copy.start()
    local[8].wait()
    w_arrive.wait_recv()
    hv_arrive.wait_recv()

    def block_rows(zb):
        return pl.ds(pl.multiple_of((zb // 4) * BR, 16), BR)

    def partials(index, zb):
        cols = pl.ds(pl.multiple_of((zb % 4) * BC, 128), BC)
        both = nn_dot(hvbuf[0], wout[0, :, cols]) + nn_dot(hvbuf[1], wout[1, :, cols])
        part[index, 0] = both[0:BR]
        part[index, 1] = both[BR : 2 * BR]

    targets_of = (dev_a2, dev_a, dev_b, dev_a, dev_b, dev_a2, dev_b2)

    def push(i):
        return pltpu.make_async_remote_copy(
            src_ref=snd.at[i], dst_ref=rcv.at[i], send_sem=r_send.at[i], recv_sem=r_recv.at[i],
            device_id=targets_of[i], device_id_type=MESH,
        )

    def send(i, value):
        snd[i] = value.astype(BF16)
        push(i).start()

    def received(i):
        push(i).wait_recv()
        return rcv[i].astype(F32)

    far, side, back = ring(4), ring(3), ring(-3)
    near_a, near_b, mid_a, mid_b = ring(1), ring(-1), ring(2), ring(-2)
    partials(0, far)
    send(0, part[0, far // 4])
    partials(1, side)
    send(1, part[1, side // 4])
    partials(2, back)
    send(2, part[2, back // 4])
    send(3, part[2, near_a // 4])
    send(4, part[1, near_b // 4])
    partials(3, mid_a)
    send(5, part[3, mid_a // 4] + received(0) + received(1))
    send(6, part[3, mid_b // 4] + received(2))
    own = part[0, z // 4] + received(3) + received(4)
    own = own + received(6)
    own = own + received(5)

    def drain_reduce():
        hv_copy.wait_send()
        for i in range(7):
            push(i).wait_send()

    ways = (dev_a, dev_a2, dev_b, dev_b2, dev_sib)

    def hid_copy(zb, way):
        return pltpu.make_async_remote_copy(
            src_ref=hid.at[c, zb], dst_ref=hid.at[c, zb], send_sem=h_send.at[zb, way],
            recv_sem=h_recv.at[c, zb], device_id=ways[way], device_id_type=MESH,
        )

    def hid_sibling(zb):
        return pltpu.make_async_remote_copy(
            src_ref=hid.at[1 - c, zb], dst_ref=hid.at[1 - c, zb], send_sem=h_send.at[zb, 4],
            recv_sem=h_recv.at[1 - c, zb], device_id=dev_sib, device_id_type=MESH,
        )

    lg[...] = jnp.zeros_like(lg)
    ss[...] = jnp.zeros_like(ss)

    def use(core, zb):
        rows = block_rows(zb)
        x = hid[core, zb]
        depth = pl.ds(pl.multiple_of(core * HALF + (zb % 4) * BC, 128), BC)
        lg[rows, :] += nn_dot(x, wvoc[depth, :])
        wide = x.astype(F32)
        square = wide * wide
        total = square[:, 0:128]
        for j in range(1, BC // 128):
            total = total + square[:, j * 128 : (j + 1) * 128]
        ss[rows, :] += total

    hid[c, z] = own.astype(BF16)
    for way in (1, 3, 0, 2, 4):
        hid_copy(z, way).start()
    local[9].wait()
    use(c, z)

    def take(zb, onward):
        hid_copy(zb, 0).wait_recv()
        for way in onward:
            hid_copy(zb, way).start()
        hid_copy(zb, 4).start()

    def use_sibling(zb):
        hid_sibling(zb).wait_recv()
        use(1 - c, zb)

    use_sibling(z)
    take(ring(-2), (1, 0))
    take(ring(2), (2,))
    use(c, ring(-2))
    use(c, ring(2))
    take(ring(-1), ())
    take(ring(1), ())
    use(c, ring(-1))
    use(c, ring(1))
    for step in (2, -2, 1, -1):
        use_sibling(ring(step))
    take(ring(-3), ())
    take(ring(3), ())
    use(c, ring(-3))
    use(c, ring(3))
    take(ring(4), ())
    use(c, ring(4))
    for step in (3, -3, 4):
        use_sibling(ring(step))

    def drain_hidden():
        for way in range(4):
            hid_copy(z, way).wait_send()
        hid_copy(ring(-2), 0).wait_send()
        hid_copy(ring(-2), 1).wait_send()
        hid_copy(ring(2), 2).wait_send()
        for zz in range(NZ):
            hid_copy(zz, 4).wait_send()

    local[10].wait()
    lane = lax.broadcasted_iota(jnp.int32, (ROWS, 128), 1)
    wide_targets = jnp.concatenate(
        [target_ref[...].astype(F32), jnp.zeros((REQ, 96), F32)], axis=1
    )
    wide_targets = jnp.concatenate([wide_targets, jnp.zeros((8 - REQ, 128), F32)], axis=0)
    turned = jnp.transpose(jnp.concatenate([wide_targets] * 16, axis=0))
    target_col = jnp.concatenate([turned[0:32, k : k + 1] for k in range(REQ)], axis=0).astype(jnp.int32)
    factor = lax.rsqrt(jnp.sum(ss[...], axis=1, keepdims=True) * (1.0 / D) + norm_epsilon)
    logits = lg[...] * factor
    top = jnp.max(logits, axis=1, keepdims=True)
    total = jnp.sum(jnp.exp(logits - top), axis=1, keepdims=True)
    hit = lax.broadcasted_iota(jnp.int32, (ROWS, VOCAB_LOCAL), 1) == target_col - t * VOCAB_LOCAL
    aimed = jnp.sum(jnp.where(hit, logits, 0.0), axis=1, keepdims=True)
    table = jnp.where(lane == 0, top, jnp.where(lane == 1, total, jnp.where(lane == 2, aimed, 0.0)))
    table = jnp.concatenate([table, jnp.zeros((128 - ROWS, 128), F32)], axis=0)
    stat[t] = jnp.transpose(table)[0:8, :]

    def stat_copy(d):
        return pltpu.make_async_remote_copy(
            src_ref=stat.at[t], dst_ref=stat.at[t], send_sem=st_send.at[d], recv_sem=st_recv.at[t],
            device_id={"tp": lax.rem(t + d, NT)}, device_id_type=MESH,
        )

    def stat_arrive(d):
        peer = lax.rem(t + d, NT)
        return pltpu.make_async_remote_copy(
            src_ref=stat.at[peer], dst_ref=stat.at[peer], send_sem=st_send.at[d], recv_sem=st_recv.at[peer],
            device_id={"tp": peer}, device_id_type=MESH,
        )

    for d in range(1, NT):
        stat_copy(d).start()

    local[11].wait()
    lane1 = lax.broadcasted_iota(jnp.int32, (1, 128), 1)
    lengths = jnp.concatenate([reply_len[...].astype(F32), jnp.zeros((REQ, 120), F32)], axis=1)
    lengths = jnp.concatenate([lengths, jnp.zeros((8 - REQ, 128), F32)], axis=0)
    sub8 = lax.broadcasted_iota(jnp.int32, (8, 128), 0)
    lane8 = lax.broadcasted_iota(jnp.int32, (8, 128), 1)
    sub128 = lax.broadcasted_iota(jnp.int32, (128, 128), 0)
    lane128 = lax.broadcasted_iota(jnp.int32, (128, 128), 1)
    to_lanes = ((lane128 % 32) // STEPS == sub128).astype(BF16)
    lengths = jnp.where(lane8 // 32 == sub8, nn_dot(lengths.astype(BF16), to_lanes), 0.0)
    lengths = jnp.sum(lengths, axis=0, keepdims=True)
    lengths = jnp.where(lane1 < ROWS, lengths, 1.0)

    drain_route()
    drain_ctx()
    drain_reduce()
    drain_hidden()
    for d in range(1, NT):
        stat_arrive(d).wait_recv()
    every = [stat[d] for d in range(NT)]
    joint = functools.reduce(jnp.maximum, [one[0:1] for one in every])
    joint_total = functools.reduce(jnp.add, [one[1:2] * jnp.exp(one[0:1] - joint) for one in every])
    joint_aimed = functools.reduce(jnp.add, [one[2:3] for one in every])
    log_prob = joint_aimed - (joint + jnp.log(joint_total))
    inside = jnp.logical_and((lane1 % STEPS).astype(F32) < lengths, lane1 < ROWS)
    value = jnp.where(inside, log_prob, 0.0) / lengths
    spread = jnp.where(lane8 // 32 == sub8, jnp.broadcast_to(value, (8, 128)), 0.0)
    pick = ((sub128 % 32) // STEPS == lane128).astype(F32)
    summed = lax.dot_general(
        spread, pick, (((1,), (0,)), ((), ())), precision=lax.Precision.HIGHEST, preferred_element_type=F32
    )
    score_ref[...] = summed[0:REQ, 0:CAND]
    for d in range(1, NT):
        stat_copy(d).wait_send()


def per_device(
    ctx_latent, ctx_rope, ctx_scale, dest, ctx_len, queries, reply_keys, reply_len, targets, w_uv, w_out, w_vocab
):
    vmem = pl.BlockSpec(memory_space=pltpu.VMEM)
    smem = pltpu.SMEM
    hbm = pl.BlockSpec(memory_space=pltpu.HBM)
    dma = pltpu.SemaphoreType.DMA
    return pl.pallas_call(
        kernel,
        out_shape=jax.ShapeDtypeStruct((REQ, CAND), F32),
        in_specs=[hbm] * 12,
        out_specs=vmem,
        scratch_shapes=[
            smem((48,), jnp.int32),
            smem((REQ,), jnp.int32),
            pltpu.VMEM((REQ, CAND), jnp.int32),
            pltpu.VMEM((REQ, 64, KVR), BF16),
            pltpu.VMEM((REQ, 32, 128), BF16),
            pltpu.VMEM((REQ, 4, 64), BF16),
            pltpu.VMEM((REQ, CAND, STEPS * KEY), BF16),
            pltpu.VMEM((REQ, 32), jnp.int32),
            pltpu.VMEM((REQ, 2, 16, WIDE_A), BF16),
            pltpu.VMEM((REQ, 2, 16, WIDE_B), BF16),
            pltpu.VMEM((2, NG, 2, 16, WIDE_A), BF16),
            pltpu.VMEM((2, NG, 2, 16, WIDE_B), BF16),
            pltpu.VMEM((NG * 2, 16, WIDE_A), BF16),
            pltpu.VMEM((NG * 2, 16, WIDE_B), BF16),
            pltpu.VMEM((NG * 2, 16, WIDE_A), BF16),
            pltpu.VMEM((NG * 2, 16, WIDE_B), BF16),
            pltpu.VMEM((2, NT, REQ, 16, WIDE_A), BF16),
            pltpu.VMEM((2, NT, REQ, 16, WIDE_B), BF16),
            pltpu.VMEM((REQ, 32, HEADS * KEY), BF16),
            pltpu.VMEM((REQ, QROWS, KVR), BF16),
            pltpu.VMEM((REQ, 2 * QROWS, 128), BF16),
            pltpu.VMEM((32, KVR), BF16),
            pltpu.VMEM((32, 128), BF16),
            pltpu.VMEM((REQ, QROWS, 1), F32),
            pltpu.VMEM((REQ, QROWS, 1), F32),
            pltpu.VMEM((REQ, QROWS, KVR), F32),
            pltpu.VMEM((HEADS, ROWS, KVR), BF16),
            pltpu.VMEM((2, ROWS, 512), BF16),
            pltpu.VMEM((KVR, 512), BF16),
            pltpu.VMEM((2, 512, HALF), BF16),
            pltpu.VMEM((D, VOCAB_LOCAL), BF16),
            pltpu.VMEM((4, 2, BR, BC), F32),
            pltpu.VMEM((7, BR, BC), BF16),
            pltpu.VMEM((7, BR, BC), BF16),
            pltpu.VMEM((2, NZ, BR, BC), BF16),
            pltpu.VMEM((ROWS, VOCAB_LOCAL), F32),
            pltpu.VMEM((ROWS, 128), F32),
            pltpu.VMEM((NT, 8, 128), F32),
            dma((12,)),
            dma((CHUNKS, NG)),
            dma((CHUNKS, NG)),
            dma((CHUNKS, NT, 3)),
            dma((CHUNKS, NT)),
            dma, dma, dma, dma,
            dma((7,)), dma((7,)),
            dma((NZ, 5)), dma((2, NZ)),
            dma((NT,)), dma((NT,)),
        ],
        compiler_params=pltpu.CompilerParams(
            collective_id=0, has_side_effects=True, vmem_limit_bytes=62 * 1024 * 1024
        ),
    )(
        dest, ctx_len, reply_len, ctx_latent, ctx_rope, jnp.swapaxes(ctx_scale, 1, 2), reply_keys, targets,
        queries, w_uv, w_out, w_vocab,
    )


def solution(mesh):
    group = ("section", "grp")
    placed = (
        P(group, "tp", None),
        P(group, "tp", None),
        P(group, "tp", None),
        P(),
        P(group),
        P(group, None, "tp"),
        P(group, None, None),
        P(group, None),
        P(group, None),
        P(None, "tp"),
        P("tp", None),
        P(None, "tp"),
    )
    return jax.shard_map(
        per_device, mesh=mesh, in_specs=placed, out_specs=P(group, None), check_vma=False
    )
```

time: 109 us -> 85.5 us (0.78)
  Pallas kernels: 97.4 us -> 84.1 us
  local copies, waits for them, and re-layouts: 10.7 us -> 1.26 us
    pallas_call x1, Pallas kernels: 97.4 us -> 84.1 us  [per_device(): pl.pallas_call(kernel, out_shape=jax.ShapeDtypeStruct((REQ, CAND), F32),...]
    unnamed x22 -> x1, local copies, waits for them, and re-layouts: 10.7 us -> 1.26 us
where the time goes in v2:
time: 85.5 us; the launch traced here: 85.4 us
  Pallas kernels  84.1 us (98%)
  local copies, waits for them, and re-layouts  1.26 us (1%)
    pallas_call x1, Pallas kernels, per_device(): pl.pallas_call(kernel, out_shape=jax.ShapeDtypeStruct((REQ, CAND), F32),...  84.1 us

profile of v2, /device:TPU:1, one launch (start us, length us, event | category | flops | bytes accessed | tf_op | source)
XLA Modules:
  0.0 85.4 jit_solution(7040839122813122396)
XLA Ops:
  0.0 84.1 %shard_map.118 = f32[3,8]{1,0:T(4,128)} custom-call(s32[48]{0:T(128)} %dest_hbm.1, s32[3]{0:T(128)} %ctx_len_hbm.1, s32[3,8]{1,0:T(4,128)} %reply_len_hbm.1, bf16[3,64,512]{2,1,0:T(8,128)(2,1)} %lat_hbm.1, bf16[3,32,128]{2,1,0:T(8,128)(2,1)} %rope_hbm.1, bf16[3,4,64]{2,1,0:T(4,128)(2,1)} %bitcast.1, bf16[3,8,2304]{2,1,0:T(8,128)(2,1)} %reply_hbm.1, ...), custom_call_target="tpu_custom_call" | custom-call | tf_op jit(solution)/shard_map/pallas_call | solution.py:513
  84.1 1.3 %copy.14 = f32[3,8]{1,0:T(4,128)} copy(f32[3,8]{1,0:T(4,128)} %shard_map.118) | data formatting | bytes 192

commit v3 on v2

--- a/solution.py
+++ b/solution.py
@@ -27,7 +27,7 @@
 ROUTE, USE = -1, -2
 SCHEDULE = (
     (1, ROUTE), (0, 0), (2, ROUTE), (1, 0), (0, 1), (3, ROUTE), (2, 0), (1, 1), (0, 2), (3, 0), (2, 1), (1, 2), (0, 3),
-    (3, 1), (2, 2), (1, 3), (0, 4), (3, 2), (2, 3), (1, 4), (0, USE), (3, 3), (2, 4), (1, USE), (3, 4), (2, USE), (3, USE),
+    (3, 1), (2, 2), (1, 3), (0, 4), (3, 2), (2, 3), (1, 4), (0, USE), (3, 3), (2, 4), (1, USE), (2, USE), (3, 4), (3, USE),
 )
 
 
@@ -345,9 +345,11 @@
     send(1, part[1, side // 4])
     partials(2, back)
     send(2, part[2, back // 4])
+    partials(3, mid_a)
+    for i in range(3):
+        push(i).wait_send()
     send(3, part[2, near_a // 4])
     send(4, part[1, near_b // 4])
-    partials(3, mid_a)
     send(5, part[3, mid_a // 4] + received(0) + received(1))
     send(6, part[3, mid_b // 4] + received(2))
     own = part[0, z // 4] + received(3) + received(4)
@@ -356,7 +358,7 @@
 
     def drain_reduce():
         hv_copy.wait_send()
-        for i in range(7):
+        for i in range(3, 7):
             push(i).wait_send()
 
     ways = (dev_a, dev_a2, dev_b, dev_b2, dev_sib)
@@ -389,8 +391,12 @@
         ss[rows, :] += total
 
     hid[c, z] = own.astype(BF16)
-    for way in (1, 3, 0, 2, 4):
+    for way in (1, 3, 4):
         hid_copy(z, way).start()
+    hid_copy(z, 1).wait_send()
+    hid_copy(z, 3).wait_send()
+    hid_copy(z, 0).start()
+    hid_copy(z, 2).start()
     local[9].wait()
     use(c, z)
 
@@ -425,8 +431,8 @@
         use_sibling(ring(step))
 
     def drain_hidden():
-        for way in range(4):
-            hid_copy(z, way).wait_send()
+        hid_copy(z, 0).wait_send()
+        hid_copy(z, 2).wait_send()
         hid_copy(ring(-2), 0).wait_send()
         hid_copy(ring(-2), 1).wait_send()
         hid_copy(ring(2), 2).wait_send()

time: 85.5 us -> 84.4 us (0.987)
  Pallas kernels: 84.1 us -> 83 us
    pallas_call x1, Pallas kernels: 84.1 us -> 83 us  [per_device(): pl.pallas_call(kernel, out_shape=jax.ShapeDtypeStruct((REQ, CAND), F32),...]
where the time goes in v3:
time: 84.4 us; the launch traced here: 84.3 us
  Pallas kernels  83 us (98%)
  local copies, waits for them, and re-layouts  1.26 us (1%)
    pallas_call x1, Pallas kernels, per_device(): pl.pallas_call(kernel, out_shape=jax.ShapeDtypeStruct((REQ, CAND), F32),...  83 us

profile of v3, /device:TPU:1, one launch (start us, length us, event | category | flops | bytes accessed | tf_op | source)
XLA Modules:
  0.0 84.3 jit_solution(9946942538268178420)
XLA Ops:
  0.0 83.0 %shard_map.118 = f32[3,8]{1,0:T(4,128)} custom-call(s32[48]{0:T(128)} %dest_hbm.1, s32[3]{0:T(128)} %ctx_len_hbm.1, s32[3,8]{1,0:T(4,128)} %reply_len_hbm.1, bf16[3,64,512]{2,1,0:T(8,128)(2,1)} %lat_hbm.1, bf16[3,32,128]{2,1,0:T(8,128)(2,1)} %rope_hbm.1, bf16[3,4,64]{2,1,0:T(4,128)(2,1)} %bitcast.1, bf16[3,8,2304]{2,1,0:T(8,128)(2,1)} %reply_hbm.1, ...), custom_call_target="tpu_custom_call" | custom-call | tf_op jit(solution)/shard_map/pallas_call | solution.py:519
  83.0 1.3 %copy.14 = f32[3,8]{1,0:T(4,128)} copy(f32[3,8]{1,0:T(4,128)} %shard_map.118) | data formatting | bytes 192

commit v4 on v3

--- a/solution.py
+++ b/solution.py
@@ -243,23 +243,27 @@
     n_col = lax.broadcasted_iota(jnp.int32, (QROWS, 256), 1)
     n_pos = (n_col // 16) * 64 + 2 * (n_col % 16)
 
-    def attend(h, k):
-        if h % 2 == 0:
-            latent = ctx_a[h // 2, :, k, :, 0:KVR].reshape(256, KVR)
-            rope_query = qr[k, 0:QROWS]
-        else:
-            latent = ctx_b[h // 2, :, k].reshape(256, KVR)
-            rope_query = qr[k, QROWS : 2 * QROWS]
-        rope = ctx_a[h // 2, :, k, :, KVR:WIDE_A].reshape(256, 128)
-        scores = (nt_dot(qn[k], latent) + nt_dot(rope_query, rope)) * softmax_scale
-        scores = jnp.where(n_pos + (h // 2) * 32 + h % 2 < ctx_len[k], scores, -jnp.inf)
-        old = m_s[k]
-        top = jnp.maximum(old, jnp.max(scores, axis=1, keepdims=True))
-        fade = jnp.exp(old - top)
-        weight = jnp.exp(scores - top)
-        m_s[k] = top
-        l_s[k] = l_s[k] * fade + jnp.sum(weight, axis=1, keepdims=True)
-        acc_s[k] = acc_s[k] * fade + nn_dot(weight.astype(BF16), latent)
+    def attend(h):
+        latent, scores = [], []
+        for k in range(REQ):
+            if h % 2 == 0:
+                latent.append(ctx_a[h // 2, :, k, :, 0:KVR].reshape(256, KVR))
+            else:
+                latent.append(ctx_b[h // 2, :, k].reshape(256, KVR))
+            rope = ctx_a[h // 2, :, k, :, KVR:WIDE_A].reshape(256, 128)
+            rope_query = qr[k, (h % 2) * QROWS : (h % 2 + 1) * QROWS]
+            one = (nt_dot(qn[k], latent[k]) + nt_dot(rope_query, rope)) * softmax_scale
+            scores.append(jnp.where(n_pos + (h // 2) * 32 + h % 2 < ctx_len[k], one, -jnp.inf))
+        old = [m_s[k] for k in range(REQ)]
+        top = [jnp.maximum(old[k], jnp.max(scores[k], axis=1, keepdims=True)) for k in range(REQ)]
+        weight = [jnp.exp(scores[k] - top[k]) for k in range(REQ)]
+        fade = [jnp.exp(old[k] - top[k]) for k in range(REQ)]
+        value = [nn_dot(weight[k].astype(BF16), latent[k]) for k in range(REQ)]
+        total = [l_s[k] * fade[k] + jnp.sum(weight[k], axis=1, keepdims=True) for k in range(REQ)]
+        for k in range(REQ):
+            m_s[k] = top[k]
+            l_s[k] = total[k]
+            acc_s[k] = acc_s[k] * fade[k] + value[k]
 
     def close_chunk(h):
         def one(zz, carry):
@@ -276,8 +280,7 @@
                 w_copy.start()
         elif i == USE:
             close_chunk(h)
-            for k in range(REQ):
-                attend(h, k)
+            attend(h)
         elif i == 0:
             open_chunk(h)
         else:

time: 84.4 us -> 82.4 us (0.976)
  Pallas kernels: 83 us -> 81.1 us
    pallas_call x1, Pallas kernels: 83 us -> 81.1 us  [per_device(): pl.pallas_call(kernel, out_shape=jax.ShapeDtypeStruct((REQ, CAND), F32),...]
where the time goes in v4:
time: 82.4 us; the launch traced here: 82.3 us
  Pallas kernels  81.1 us (98%)
  local copies, waits for them, and re-layouts  1.26 us (2%)
    pallas_call x1, Pallas kernels, per_device(): pl.pallas_call(kernel, out_shape=jax.ShapeDtypeStruct((REQ, CAND), F32),...  81.1 us

profile of v4, /device:TPU:1, one launch (start us, length us, event | category | flops | bytes accessed | tf_op | source)
XLA Modules:
  0.0 82.3 jit_solution(17407238072115702900)
XLA Ops:
  0.0 81.1 %shard_map.118 = f32[3,8]{1,0:T(4,128)} custom-call(s32[48]{0:T(128)} %dest_hbm.1, s32[3]{0:T(128)} %ctx_len_hbm.1, s32[3,8]{1,0:T(4,128)} %reply_len_hbm.1, bf16[3,64,512]{2,1,0:T(8,128)(2,1)} %lat_hbm.1, bf16[3,32,128]{2,1,0:T(8,128)(2,1)} %rope_hbm.1, bf16[3,4,64]{2,1,0:T(4,128)(2,1)} %bitcast.1, bf16[3,8,2304]{2,1,0:T(8,128)(2,1)} %reply_hbm.1, ...), custom_call_target="tpu_custom_call" | custom-call | tf_op jit(solution)/shard_map/pallas_call | solution.py:522
  81.1 1.3 %copy.14 = f32[3,8]{1,0:T(4,128)} copy(f32[3,8]{1,0:T(4,128)} %shard_map.118) | data formatting | bytes 192

commit v5 on v4

--- a/solution.py
+++ b/solution.py
@@ -381,17 +381,22 @@
     lg[...] = jnp.zeros_like(lg)
     ss[...] = jnp.zeros_like(ss)
 
-    def use(core, zb):
-        rows = block_rows(zb)
-        x = hid[core, zb]
-        depth = pl.ds(pl.multiple_of(core * HALF + (zb % 4) * BC, 128), BC)
-        lg[rows, :] += nn_dot(x, wvoc[depth, :])
-        wide = x.astype(F32)
-        square = wide * wide
-        total = square[:, 0:128]
-        for j in range(1, BC // 128):
-            total = total + square[:, j * 128 : (j + 1) * 128]
-        ss[rows, :] += total
+    def use(core, *blocks):
+        products, squares = [], []
+        for zb in blocks:
+            x = hid[core, zb]
+            depth = pl.ds(pl.multiple_of(core * HALF + (zb % 4) * BC, 128), BC)
+            products.append(nn_dot(x, wvoc[depth, :]))
+            wide = x.astype(F32)
+            square = wide * wide
+            total = square[:, 0:128]
+            for j in range(1, BC // 128):
+                total = total + square[:, j * 128 : (j + 1) * 128]
+            squares.append(total)
+        for zb, product, square in zip(blocks, products, squares):
+            rows = block_rows(zb)
+            lg[rows, :] += product
+            ss[rows, :] += square
 
     hid[c, z] = own.astype(BF16)
     for way in (1, 3, 4):
@@ -426,12 +431,11 @@
         use_sibling(ring(step))
     take(ring(-3), ())
     take(ring(3), ())
-    use(c, ring(-3))
-    use(c, ring(3))
     take(ring(4), ())
-    use(c, ring(4))
+    use(c, ring(-3), ring(3), ring(4))
     for step in (3, -3, 4):
-        use_sibling(ring(step))
+        hid_sibling(ring(step)).wait_recv()
+    use(1 - c, ring(3), ring(-3), ring(4))
 
     def drain_hidden():
         hid_copy(z, 0).wait_send()

time: 82.4 us -> 82.4 us (level)
  no operation moved by 1% of the time
where the time goes in v5:
time: 82.4 us; the launch traced here: 82.3 us
  Pallas kernels  81 us (98%)
  local copies, waits for them, and re-layouts  1.26 us (2%)
    pallas_call x1, Pallas kernels, per_device(): pl.pallas_call(kernel, out_shape=jax.ShapeDtypeStruct((REQ, CAND), F32),...  81 us

profile of v5, /device:TPU:1, one launch (start us, length us, event | category | flops | bytes accessed | tf_op | source)
XLA Modules:
  0.0 82.3 jit_solution(16275360582753124901)
XLA Ops:
  0.0 81.0 %shard_map.118 = f32[3,8]{1,0:T(4,128)} custom-call(s32[48]{0:T(128)} %dest_hbm.1, s32[3]{0:T(128)} %ctx_len_hbm.1, s32[3,8]{1,0:T(4,128)} %reply_len_hbm.1, bf16[3,64,512]{2,1,0:T(8,128)(2,1)} %lat_hbm.1, bf16[3,32,128]{2,1,0:T(8,128)(2,1)} %rope_hbm.1, bf16[3,4,64]{2,1,0:T(4,128)(2,1)} %bitcast.1, bf16[3,8,2304]{2,1,0:T(8,128)(2,1)} %reply_hbm.1, ...), custom_call_target="tpu_custom_call" | custom-call | tf_op jit(solution)/shard_map/pallas_call | solution.py:526
  81.0 1.3 %copy.14 = f32[3,8]{1,0:T(4,128)} copy(f32[3,8]{1,0:T(4,128)} %shard_map.118) | data formatting | bytes 192
